TPU v7x, 32 devices: a whole 2x2x4 slice. The times are simulated.
32 devices in a mesh: img: 8 (over z, x), row: 4 (over y, core).
Axes of the slice: x: 2, y: 2, z: 4, core: 2. Of those that a mesh axis runs over, the one named last changes fastest.
Arguments:
- tokens: bfloat16 [16, 24, 24, 768], P('img', 'row'), may hold values from -6 to 6
- keep_mask: int32 [16, 24, 24], P('img', 'row'), may hold values from 0 to 1, as said below
- cotangent: bfloat16 [16, 24, 24, 768], P('img', 'row'), may hold values from -6 to 6
- qkv_weight: float32 [768, 2304], P('img', 'row'), may hold values from -0.21875 to 0.21875
- qkv_bias: float32 [2304], P(('img', 'row')), may hold values from -1.5 to 1.5
- proj_weight: float32 [768, 768], P('img', 'row'), may hold values from -1.75 to 1.75
- proj_bias: float32 [768], P(('img', 'row')), may hold values from -1.5 to 1.5
- attn_gain: float32 [768], P(('img', 'row')), may hold values from 0.1 to 1.9
- attn_shift: float32 [768], P(('img', 'row')), may hold values from -1.5 to 1.5
- mlp_gain: float32 [768], P(('img', 'row')), may hold values from 0.1 to 1.9
- mlp_shift: float32 [768], P(('img', 'row')), may hold values from -1.5 to 1.5
- up_weight: float32 [768, 3072], P('img', 'row'), may hold values from -0.21875 to 0.21875
- up_bias: float32 [3072], P(('img', 'row')), may hold values from -1.5 to 1.5
- down_weight: float32 [3072, 768], P('row', 'img'), may hold values from -0.109375 to 0.109375
- down_bias: float32 [768], P(('img', 'row')), may hold values from -1.5 to 1.5
- rope_freqs: float32 [768], P(('img', 'row')), may hold values from -1 to 1
Outputs:
- layer_out: bfloat16 [16, 24, 24, 768], P('img', 'row')
- tokens_grad: bfloat16 [16, 24, 24, 768], P('img', 'row')
- qkv_weight_grad: float32 [768, 2304], P('img', 'row')
- qkv_bias_grad: float32 [1536], P(('img', 'row'))
- value_bias_grad: float32 [768], P(('img', 'row'))
- proj_weight_grad: float32 [768, 768], P('img', 'row')
- proj_bias_grad: float32 [768], P(('img', 'row'))
- attn_gain_grad: float32 [768], P(('img', 'row'))
- attn_shift_grad: float32 [768], P(('img', 'row'))
- mlp_gain_grad: float32 [768], P(('img', 'row'))
- mlp_shift_grad: float32 [768], P(('img', 'row'))
- up_weight_grad: float32 [768, 3072], P('img', 'row')
- up_bias_grad: float32 [3072], P(('img', 'row'))
- down_weight_grad: float32 [3072, 768], P('row', 'img')
- down_bias_grad: float32 [768], P(('img', 'row'))
- rope_freqs_grad: float32 [768], P(('img', 'row'))
Inputs may be any that keep to these rules, and one draw needn't show every extreme that they name: `keep_mask`: every image keeps all patches of one grid column drawn for it; each of its other patches is kept with one probability drawn per image from 1, 1/2, 1/4, 1/8, 1/16, 1/32.
All inputs are finite; a program needn't handle non-finite values.
Results may differ from a plain program's by a relative error of at most 0.018.
The roundings to bfloat16 on the way count: a program that leaves them out, or rounds other values in their place, can miss the bound.
Values may be sent and summed in bfloat16 or wider, within the bound.
No kernel may reach another device: no remote copies, remote signals or barrier semaphores. Data moves between devices by JAX's collectives and lax.ppermute only.
A program may use at most 192 MiB of HBM per device.

v0:
```python
import functools

import jax
import jax.numpy as jnp
import numpy as np
from jax import lax
from jax.experimental import pallas as pl
from jax.experimental.pallas import tpu as pltpu
from jax.sharding import PartitionSpec as P

HEADS = 12
NORM_EPSILON = 1e-06
MASKED_SCORE = -1e30
BF = jnp.bfloat16
F32 = jnp.float32
MIB = 2**20
VMEM = pl.BlockSpec(memory_space=pltpu.VMEM)
SMEM = pl.BlockSpec(memory_space=pltpu.SMEM)


def dot(left, right, dims):
    return lax.dot_general(left, right, (dims, ((), ())), preferred_element_type=F32)


def nn(left, right):
    return dot(left, right, ((1,), (0,)))


def nt(left, right):
    return dot(left, right, ((1,), (1,)))


def tn(left, right):
    return dot(left, right, ((0,), (0,)))


def normed_rows(values):
    center = values - jnp.mean(values, -1, keepdims=True)
    inverse = lax.rsqrt(jnp.mean(center * center, -1, keepdims=True) + NORM_EPSILON)
    return center * inverse, inverse


def norm_back(grad, normed, inverse, gain):
    scaled = grad * gain
    centred = scaled - jnp.mean(scaled, -1, keepdims=True)
    return inverse * (centred - normed * jnp.mean(scaled * normed, -1, keepdims=True))


def column_sum(value):
    return jnp.sum(value, 0, keepdims=True)


class Layout:
    def __init__(self, img_count, tokens, rows):
        self.img_count = img_count
        self.bits = img_count.bit_length() - 1
        self.rows = rows
        self.half_rows = rows // 2
        self.aligned = rows % 32 == 0
        self.images, self.band_rows, self.side, self.width = tokens.shape
        self.band = self.band_rows * self.side
        self.length = 4 * self.band
        self.head = self.width // HEADS
        self.own = self.width // 2
        self.third = self.own // 2
        self.high = list(range(self.bits - 1, 0, -1))
        self.tiles = (img_count, rows) if self.aligned else (1, self.width)

    def slots(self, img_rel, y_rel):
        high = 0
        for k, bit in enumerate(self.high):
            high = high + (((img_rel >> bit) & 1) << k)
        top = self.bits - 1
        return (high + ((img_rel & 1) << top), y_rel), (high + (y_rel << top), img_rel & 1)


def load_pieces(lay, me_ref, refs, y_rel, target):
    if not lay.aligned:
        target[...] = refs[0][me_ref[1] ^ y_rel]
        return
    half = lay.half_rows
    base = lay.img_count // 2
    for img_rel in range(lay.img_count):
        for part, (slot, last) in enumerate(lay.slots(img_rel, y_rel)):
            ref = refs[4 * part + 2 * last + slot // base]
            target[img_rel ^ me_ref[0], part * half : (part + 1) * half] = ref[slot % base]


def store_pieces(lay, me_ref, refs, y_rel, columns, source):
    if not lay.aligned:
        refs[0][me_ref[1] ^ y_rel, :, :, columns] = source[...]
        return
    half = lay.half_rows
    for img_rel in range(lay.img_count):
        for part, (slot, last) in enumerate(lay.slots(img_rel, y_rel)):
            refs[2 * part + last][slot, :, columns] = source[img_rel ^ me_ref[0], part * half : (part + 1) * half]


def halves_of(lay, value):
    pairs = lay.head // 2
    lane = lax.broadcasted_iota(jnp.int32, value.shape, 1)
    width = value.shape[1]
    first = (lane & pairs) == 0
    return jnp.where(first, pltpu.roll(value, width - pairs, 1), pltpu.roll(value, pairs, 1))


def pack_kernel(lay, me_ref, tok_ref, cot_ref, mask_ref, qkv_ref, proj_ref, up_ref, down_ref, *refs):
    vectors = refs[:9]
    mine_ref, other_ref, third_ref, first_ref, second_ref = refs[9:]
    y = me_ref[1]
    band, third, width = lay.band, lay.third, lay.width
    third_ref[:, :third] = qkv_ref[:, third : 2 * third].astype(BF)
    third_ref[:, third:] = jnp.zeros((lay.rows, third_ref.shape[1] - third), BF)
    first_ref[:, :third] = qkv_ref[:, :third].astype(BF)
    first_ref[:, third : 2 * third] = qkv_ref[:, 2 * third :].astype(BF)
    first_ref[:, 2 * third :] = proj_ref[...].astype(BF)
    second_ref[:, :width] = up_ref[...].astype(BF)
    second_ref[:, width:] = down_ref[...].astype(BF)
    packed = jnp.concatenate([v[...] for v in vectors], 1)
    packed = jnp.concatenate([packed, jnp.zeros((1, width - packed.shape[1]), F32)], 1)
    for ref, which in ((mine_ref, y), (other_ref, 1 - y)):
        ref[:band] = tok_ref[which]
        ref[band : 2 * band] = cot_ref[which]
        keep = mask_ref[which].astype(F32)
        flat = jnp.concatenate([keep[r : r + 1] for r in range(lay.band_rows)], 1)
        flat = jnp.concatenate([flat, jnp.zeros((1, width - band), F32)], 1)
        ref[2 * band :] = jnp.concatenate([flat, packed, jnp.zeros((14, width), F32)], 0).astype(BF)


def fit_kernel(lay, me_ref, came_ref, first_ref, out_ref):
    third = lay.third
    c = me_ref[2]
    t0, t2, came = first_ref[:, :third], first_ref[:, third : 2 * third], came_ref[:, :third]
    out_ref[:, : 3 * third] = jnp.where(c == 0, jnp.concatenate([t0, t2, came], 1), jnp.concatenate([came, t0, t2], 1))
    out_ref[:, 3 * third :] = first_ref[:, 2 * third :]


def merge_kernel(lay, *refs):
    pieces, (top_ref, bottom_ref) = refs[:-2], refs[-2:]
    half = lay.half_rows
    for k, ref in enumerate(pieces):
        top_ref[k] = ref[:half]
        bottom_ref[k] = ref[half:]


def owner_mask(lay, devices, table_row, me_ref):
    place = lax.broadcasted_iota(jnp.int32, (devices, 1), 0)
    row_rel, img_place = place & 3, place >> 2
    row = (((row_rel & 1) << 1) | (row_rel >> 1)) ^ me_ref[3]
    img_rel = jnp.zeros_like(place)
    for k, bit in enumerate(lay.high + [0]):
        img_rel = img_rel | (((img_place >> k) & 1) << bit)
    return ((img_rel ^ me_ref[0]) * 4 + row) == table_row


def unpack_kernel(lay, plan, me_ref, v_ref, table_ref, out_ref):
    c = me_ref[2]
    devices = v_ref.shape[0]
    for start, size, offset, count in plan:
        at = slice(start, start + size)
        owner = jnp.where(c == 0, table_ref[0:1, at], table_ref[2:3, at])
        entry = jnp.where(c == 0, table_ref[1:2, at], table_ref[3:4, at])
        place = lax.broadcasted_iota(jnp.int32, (count, size), 0)
        spread = (place == entry).astype(F32).astype(BF)
        rows = nn(v_ref[:, offset : offset + count], spread)
        out_ref[:, at] = column_sum(jnp.where(owner_mask(lay, devices, owner, me_ref), rows, 0.0))


def repack_kernel(lay, plan, me_ref, table_ref, *refs):
    grads, out_ref = refs[:-1], refs[-1]
    c = me_ref[2]
    devices = out_ref.shape[0]
    out_ref[...] = jnp.zeros_like(out_ref)
    for ref, (start, size, offset, count) in zip(grads, plan):
        at = slice(start, start + size)
        owner = jnp.where(c == 0, table_ref[0:1, at], table_ref[2:3, at])
        entry = jnp.where(c == 0, table_ref[1:2, at], table_ref[3:4, at])
        place = lax.broadcasted_iota(jnp.int32, (count, size), 0)
        spread = (place == entry).astype(F32).astype(BF)
        rows = jnp.where(owner_mask(lay, devices, owner, me_ref), ref[...], 0.0).astype(BF)
        out_ref[:, offset : offset + count] = nt(rows, spread)


def project_kernel(lay, n_w, me_ref, t0, t1, t2, t3, *refs):
    w_refs = refs[:n_w]
    vec_ref, a_ref, q_ref, k_ref, v_ref, w_out, p_out, cos_ref, sin_ref, kp_ref, bias_ref, w_all = refs[n_w:]
    band, side, own, third = lay.band, lay.side, lay.own, lay.third
    g_ref, s_ref, b_ref = (vec_ref[:, lay.at[n]] for n in ("attn_gain", "attn_shift", "qkv_bias"))
    f_ref = vec_ref[:, lay.at["freqs"]]
    keeps = []
    for b, ref in enumerate((t0, t1, t2, t3)):
        at = slice(b * band, (b + 1) * band)
        normed, _ = normed_rows(ref[:band].astype(F32))
        a_ref[at] = (normed * g_ref + s_ref).astype(BF)
        keep = ref[2 * band :, :band].astype(F32)
        kp_ref[at] = jnp.transpose(keep)[:, 0:1]
        keeps.append(keep[0:1])
    bias_ref[...] = jnp.where(jnp.concatenate(keeps, 1) > 0, 0.0, MASKED_SCORE)
    lane = lax.broadcasted_iota(jnp.int32, (side, own), 1)
    sign = jnp.where((lane & (lay.head // 2)) == 0, -1.0, 1.0).astype(F32)
    col = lax.broadcasted_iota(jnp.int32, (side, own), 0).astype(F32) * f_ref[:, :own]
    col_cos, col_sin = jnp.cos(col), jnp.sin(col)
    row_index = me_ref[3]
    for b, flip in enumerate((0, 2, 1, 3)):
        first = ((row_index ^ flip) * lay.band_rows).astype(F32)
        rows = (lax.broadcasted_iota(jnp.int32, (8, own), 0).astype(F32) + first) * f_ref[:, own:]
        row_cos, row_sin = jnp.cos(rows), jnp.sin(rows)
        for r in range(lay.band_rows):
            at = slice(b * band + r * side, b * band + (r + 1) * side)
            rc, rs = row_cos[r : r + 1], row_sin[r : r + 1]
            cos_ref[at] = col_cos * rc - col_sin * rs
            sin_ref[at] = (col_sin * rc + col_cos * rs) * sign
    block = lay.width // 4
    for y_rel in range(2):
        y_side = me_ref[1] ^ y_rel
        load_pieces(lay, me_ref, w_refs, y_rel, w_all.at[y_side])
    acts = a_ref[...]
    w0, w1 = w_all[0].reshape(lay.width, -1), w_all[1].reshape(lay.width, -1)
    p_out[:, :block], p_out[:, block:] = w0[:, 3 * third :], w1[:, 3 * third :]
    w0, w1 = w0[:, : 3 * third], w1[:, : 3 * third]
    w_out[0], w_out[1] = w0, w1
    left = nn(acts, w0) + b_ref[:, : 3 * third]
    right = nn(acts, w1) + b_ref[:, 3 * third :]
    query, key = left[:, :own], jnp.concatenate([left[:, own:], right[:, :third]], 1)
    cos, sin = cos_ref[...], sin_ref[...]
    q_ref[...] = (query * cos + halves_of(lay, query) * sin).astype(BF)
    k_ref[...] = (key * cos + halves_of(lay, key) * sin).astype(BF)
    v_ref[...] = right[:, third:].astype(BF)


def attend_kernel(lay, chunk, q_ref, k_ref, v_ref, bias_ref, o_ref, p_ref):
    head = lay.head
    pair = 2 * head
    scale = head**-0.5

    def step(n, carry):
        at = pl.ds(pl.multiple_of(n * pair, pair), pair)
        keys, values = k_ref[:, at], v_ref[:, at]
        for start in range(0, lay.length, chunk):
            rows = slice(start, start + chunk)
            query = q_ref[rows, at] * jnp.asarray(scale, BF)
            lane = lax.broadcasted_iota(jnp.int32, query.shape, 1)
            outs = []
            for h in range(2):
                mine = (lane < head) if h == 0 else (lane >= head)
                score = nt(jnp.where(mine, query, jnp.zeros_like(query)), keys) + bias_ref[...]
                power = jnp.exp(score - jnp.max(score, -1, keepdims=True))
                weights = (power * (1.0 / jnp.sum(power, -1, keepdims=True))).astype(BF)
                p_ref[2 * n + h, rows] = weights
                outs.append(nn(weights, values))
            o_ref[rows, at] = jnp.where(lane < head, outs[0], outs[1]).astype(BF)
        return carry

    lax.fori_loop(0, HEADS // 4, step, 0)


def middle_kernel(lay, me_ref, t0, t1, t2, t3, ob_ref, oo_ref, p_ref, po_ref, vec_ref, x1_ref, a2_ref, wp_ref):
    band, third, half = lay.band, lay.third, lay.length // 2
    c = me_ref[2]
    block = lay.width // 4
    pb_ref, g_ref, s_ref = (vec_ref[:, lay.at[n]] for n in ("proj_bias", "mlp_gain", "mlp_shift"))
    for y_side in range(2):
        mine, other = (ref[:, y_side * block : (y_side + 1) * block] for ref in (p_ref, po_ref))
        wp_ref[:, 2 * y_side * block : 2 * (y_side + 1) * block] = jnp.where(
            c == 0, jnp.concatenate([mine, other], 1), jnp.concatenate([other, mine], 1)
        )
    low = [pl.ds(pl.multiple_of((2 * s + c) * third, third), third) for s in range(2)]
    high = [pl.ds(pl.multiple_of((2 * s + 1 - c) * third, third), third) for s in range(2)]
    own_w = jnp.concatenate([wp_ref[low[0]], wp_ref[low[1]]], 0)
    other_w = jnp.concatenate([wp_ref[high[0]], wp_ref[high[1]]], 0)
    other = jnp.concatenate([oo_ref[half:], oo_ref[:half]], 0)
    x1_ref[...] = nn(ob_ref[...], own_w) + nn(other, other_w) + pb_ref
    for b, ref in enumerate((t0, t1, t2, t3)):
        at = slice(b * band, (b + 1) * band)
        x1 = x1_ref[at] + ref[:band].astype(F32)
        x1_ref[at] = x1
        normed, _ = normed_rows(x1)
        a2_ref[at] = (normed * g_ref + s_ref).astype(BF)


def mlp_kernel(lay, n_w, n_g, chunk, me_ref, t0, t1, t2, t3, kp_ref, x1_ref, a2_ref, *refs):
    w_refs = refs[:n_w]
    vec_ref, part_ref, msend_ref, dn_ref, dnsend_ref, ubg_ref, dbg_ref = refs[n_w : n_w + 7]
    grads = refs[n_w + 7 : n_w + 7 + n_g]
    dm_ref, at_ref, dt_ref, m_ref, w_all, g_tmp = refs[n_w + 7 + n_g :]
    band, width, half = lay.band, lay.width, lay.length // 2
    up_bias = lay.at["up_bias"].start
    for b, ref in enumerate((t0, t1, t2, t3)):
        at = slice(b * band, (b + 1) * band)
        dm_ref[at] = (ref[band : 2 * band].astype(F32) * kp_ref[at]).astype(BF)
    at_ref[...] = a2_ref[...].T
    dt_ref[...] = dm_ref[...].T
    dbg_ref[...] = column_sum(dm_ref[:half].astype(F32))
    m_ref[...] = jnp.zeros_like(m_ref)
    dn_ref[...] = jnp.zeros_like(dn_ref)
    shape = lay.tiles + (chunk,)

    for y_rel in range(2):
        load_pieces(lay, me_ref, w_refs, y_rel, w_all)

        def step(n, carry, y_rel=y_rel):
            at = pl.ds(pl.multiple_of(n * chunk, chunk), chunk)
            d_at = pl.ds(pl.multiple_of(n * chunk + width, chunk), chunk)
            b_at = n * chunk + (me_ref[1] ^ y_rel) * width
            up = w_all[:, :, at].reshape(width, chunk)
            down = w_all[:, :, d_at].reshape(width, chunk)
            acts = a2_ref[...]
            dm = dm_ref[...]
            pre = nn(acts, up) + vec_ref[:, pl.ds(pl.multiple_of(b_at + up_bias, 128), chunk)]
            cdf = 0.5 * (1.0 + lax.erf(pre * 0.7071067811865476))
            slope = cdf + pre * (jnp.exp(-0.5 * pre * pre) * 0.3989422804014327)
            act = (pre * cdf).astype(BF)
            du = (nn(dm, down) * slope).astype(BF)
            ubg_ref[:, pl.ds(pl.multiple_of(b_at, chunk), chunk)] = column_sum(du.astype(F32))
            m_ref[...] += nt(act, down)
            dn_ref[...] += nt(du, up)
            g_tmp[...] = nn(at_ref[...], du).astype(BF).reshape(shape)
            store_pieces(lay, me_ref, grads, y_rel, at, g_tmp)
            g_tmp[...] = nn(dt_ref[...], act).astype(BF).reshape(shape)
            store_pieces(lay, me_ref, grads, y_rel, d_at, g_tmp)
            return carry

        lax.fori_loop(0, width // chunk, step, 0)
    part_ref[...] = x1_ref[:half] + m_ref[:half] + vec_ref[:, lay.at["down_bias"]]
    msend_ref[...] = m_ref[half:].astype(BF)
    dnsend_ref[...] = dn_ref[...].astype(BF)


def back_kernel(
    lay, n_g, chunk, me_ref, t0, t1, t2, t3, kp_ref, x1_ref, dn_ref, came_ref, vec_ref, wp_ref, ob_ref, oo_ref, q_ref, k_ref, v_ref,
    p_ref, cos_ref, sin_ref, a_ref, *refs,
):
    dx_ref, pbg_ref, gg_ref, sg_ref, bqk_ref, bv_ref, fg_ref, dqkv_ref = refs[:8]
    grads = refs[8 : 8 + n_g]
    dxb_ref, dob_ref, dq_ref, dk_ref, dv_ref, g_tmp = refs[8 + n_g :]
    g_ref = vec_ref[:, lay.at["mlp_gain"]]
    band, side, own, third, half, head = lay.band, lay.side, lay.own, lay.third, lay.length // 2, lay.head
    c = me_ref[2]
    pair = 2 * head
    scale = head**-0.5
    gg, sg, pbg = 0.0, 0.0, 0.0
    for b, ref in enumerate((t0, t1, t2, t3)):
        at = slice(b * band, (b + 1) * band)
        away = slice((b ^ 2) * band, ((b ^ 2) + 1) * band)
        dn = dn_ref[at] + came_ref[away].astype(F32)
        normed, inverse = normed_rows(x1_ref[at])
        dx = ref[band : 2 * band].astype(F32) * kp_ref[at] + norm_back(dn, normed, inverse, g_ref)
        dxb = dx.astype(BF)
        dxb_ref[at] = dxb
        if b < 2:
            dx_ref[at] = dx
            gg = gg + column_sum(dn * normed)
            sg = sg + column_sum(dn)
            pbg = pbg + column_sum(dxb.astype(F32))
    gg_ref[...], sg_ref[...], pbg_ref[...] = gg, sg, pbg
    low = [pl.ds(pl.multiple_of((2 * s + c) * third, third), third) for s in range(2)]
    own_w = jnp.concatenate([wp_ref[low[0]], wp_ref[low[1]]], 0)
    dxb = dxb_ref[...]
    dob_ref[...] = nt(dxb, own_w).astype(BF)
    block = lay.width // 4
    zero = jnp.concatenate([dxb[:, :block], dxb[:, 2 * block : 3 * block]], 1)
    one = jnp.concatenate([dxb[:, block : 2 * block], dxb[:, 3 * block :]], 1)
    cols = jnp.where(c == 0, zero, one)
    other = jnp.concatenate([oo_ref[half:], oo_ref[:half]], 0)
    mine_g, other_g = tn(ob_ref[...], cols).astype(BF), tn(other, cols).astype(BF)
    zero, one = jnp.where(c == 0, mine_g, other_g), jnp.where(c == 0, other_g, mine_g)
    p_grad = jnp.concatenate([zero[:third], one[:third], zero[third:], one[third:]], 0)

    def step(n, carry):
        at = pl.ds(pl.multiple_of(n * pair, pair), pair)
        keys, values = k_ref[:, at], v_ref[:, at]
        for start in range(0, lay.length, chunk):
            rows = slice(start, start + chunk)
            query, dob = q_ref[rows, at], dob_ref[rows, at]
            lane = lax.broadcasted_iota(jnp.int32, query.shape, 1)
            dqs, dks, dvs = [], [], []
            for h in range(2):
                mine = (lane < head) if h == 0 else (lane >= head)
                weights = p_ref[2 * n + h, rows]
                soft = weights.astype(F32)
                dp = nt(jnp.where(mine, dob, jnp.zeros_like(dob)), values)
                ds = (soft * (dp - jnp.sum(soft * dp, -1, keepdims=True))).astype(BF)
                dqs.append(nn(ds, keys))
                dks.append(tn(ds, query))
                dvs.append(tn(weights, dob))
            dq_ref[rows, at] = jnp.where(lane < head, dqs[0], dqs[1]) * scale
            lane = lax.broadcasted_iota(jnp.int32, keys.shape, 1)
            dk = jnp.where(lane < head, dks[0], dks[1]) * scale
            dv = jnp.where(lane < head, dvs[0], dvs[1])
            if start == 0:
                dk_ref[:, at] = dk
                dv_ref[:, at] = dv
            else:
                dk_ref[:, at] += dk
                dv_ref[:, at] += dv
        return carry

    lax.fori_loop(0, HEADS // 4, step, 0)
    cos, sin = cos_ref[...], sin_ref[...]
    dq, dk = dq_ref[...], dk_ref[...]
    dqkv_ref[:, :own] = (dq * cos + halves_of(lay, dq * sin)).astype(BF)
    dqkv_ref[:, own : 2 * own] = (dk * cos + halves_of(lay, dk * sin)).astype(BF)
    dqkv_ref[:, 2 * own :] = dv_ref[...].astype(BF)
    dq_ref[...] = dq * halves_of(lay, q_ref[...].astype(F32)) + dk * halves_of(lay, k_ref[...].astype(F32))
    by_col = jnp.zeros((side, own), F32)
    by_row = jnp.zeros((side, own), F32)
    for b, flip in enumerate((0, 2, 1, 3)):
        first = ((me_ref[3] ^ flip) * lay.band_rows).astype(F32)
        for r in range(lay.band_rows):
            turn = dq_ref[b * band + r * side : b * band + (r + 1) * side]
            by_col = by_col + turn
            by_row = by_row + turn * (first + r)
    lane = lax.broadcasted_iota(jnp.int32, (2, own), 1)
    sign = jnp.where((lane & (head // 2)) == 0, -1.0, 1.0).astype(F32)
    place = lax.broadcasted_iota(jnp.int32, (side, own), 0).astype(F32)
    both = jnp.concatenate([column_sum(by_col * place), column_sum(by_row)], 0) * sign
    both = jnp.where(sign < 0, both + halves_of(lay, both), 0.0)
    fg_ref[:, :own], fg_ref[:, own:] = both[0:1], both[1:2]
    bqk_ref[...] = column_sum(dqkv_ref[:, : 2 * own].astype(F32))
    bv_ref[...] = column_sum(dqkv_ref[:, 2 * own :].astype(F32))
    acts = a_ref[...]
    sides = []
    for y_side in range(2):
        grad = tn(acts, dqkv_ref[:, y_side * 3 * third : (y_side + 1) * 3 * third]).astype(BF)
        sides.append(jnp.concatenate([grad, p_grad[:, y_side * block : (y_side + 1) * block]], 1))
    y = me_ref[1]
    for y_rel in range(2):
        g_tmp[...] = jnp.where((y ^ y_rel) == 0, sides[0], sides[1]).reshape(g_tmp.shape)
        store_pieces(lay, me_ref, grads, y_rel, slice(None), g_tmp)


def last_kernel(lay, dqkv_ref, w_ref, keep_ref, send_ref):
    third, half = lay.third, lay.length // 2
    grad = nt(dqkv_ref[:, : 3 * third], w_ref[0]) + nt(dqkv_ref[:, 3 * third :], w_ref[1])
    keep_ref[...] = grad[:half]
    send_ref[...] = grad[half:].astype(BF)


def finish_kernel(lay, t0, t1, keep_ref, came_ref, dx_ref, vec_ref, out_ref, send_ref, gg_ref, sg_ref):
    band = lay.band
    g_ref = vec_ref[:, lay.at["attn_gain"]]
    gg, sg = 0.0, 0.0
    for b, ref in enumerate((t0, t1)):
        at = slice(b * band, (b + 1) * band)
        dn = keep_ref[at] + came_ref[at].astype(F32)
        normed, inverse = normed_rows(ref[:band].astype(F32))
        result = (dx_ref[at] + norm_back(dn, normed, inverse, g_ref)).astype(BF)
        if b == 0:
            out_ref[...] = result
        else:
            send_ref[...] = result
        gg = gg + column_sum(dn * normed)
        sg = sg + column_sum(dn)
    gg_ref[...], sg_ref[...] = gg, sg


def call(kernel, name, inputs, outs, scratch=(), smem=1, limit=16, us=1):
    return pl.pallas_call(
        kernel,
        out_shape=[jax.ShapeDtypeStruct(shape, dtype) for shape, dtype in outs],
        in_specs=[SMEM] * smem + [VMEM] * (len(inputs) - smem),
        out_specs=[VMEM] * len(outs),
        scratch_shapes=[pltpu.VMEM(shape, dtype) for shape, dtype in scratch],
        compiler_params=pltpu.CompilerParams(vmem_limit_bytes=limit * MIB),
        cost_estimate=pl.CostEstimate(flops=us * 1000000000, bytes_accessed=1024, transcendentals=0),
        name=name,
    )(*inputs)


class Slice:
    def __init__(self, lay):
        self.lay = lay
        self.img = lax.axis_index("img")
        self.row = lax.axis_index("row")
        self.y = self.row // 2
        self.c = self.row % 2
        self.facts = jnp.stack([self.img, self.y, self.c, self.row]).astype(jnp.int32)
        self.orders = (lay.high + [0, "y"], lay.high + ["y", 0])

    def swap(self, array, step):
        if step == "c":
            return lax.ppermute(array, "row", [(r, r ^ 1) for r in range(4)])
        if step == "y":
            return lax.ppermute(array, "row", [(r, r ^ 2) for r in range(4)])
        return lax.ppermute(array, "img", [(i, i ^ (1 << step)) for i in range(self.lay.img_count)])

    def gather(self, piece, order):
        held = piece[None]
        for step in order:
            held = jnp.concatenate([held, self.swap(held, step)], 0)
        return held

    def scatter(self, held, order):
        for step in reversed(order):
            half = held.shape[0] // 2
            came = self.swap(held[half:], step)
            held = (held[:half].astype(F32) + came.astype(F32)).astype(held.dtype)
        return held[0]

    def places(self, order):
        place = jnp.zeros((2, self.lay.img_count), jnp.int32)
        img = jnp.arange(self.lay.img_count, dtype=jnp.int32)[None, :] ^ self.img
        side = jnp.arange(2, dtype=jnp.int32)[:, None] ^ self.y
        for k, step in enumerate(order):
            bit = side if step == "y" else (img >> step) & 1
            place = place + (bit << k)
        return place

    def sources(self, order):
        place = self.places(order).reshape(-1)
        return jnp.zeros_like(place).at[place].set(jnp.arange(place.size, dtype=jnp.int32))

    def gather_rows(self, piece, name):
        lay = self.lay
        if not lay.aligned:
            base = self.gather(piece, lay.high)
            whole = []
            for part, order in enumerate(self.orders):
                held = base[:, part * lay.half_rows : (part + 1) * lay.half_rows]
                held = self.gather(held, order[-2:]).reshape((-1,) + held.shape[1:])
                whole.append(jnp.take(held, self.places(order), axis=0))
            return [jnp.concatenate(whole, 2).reshape((2,) + lay.tiles + piece.shape[1:])]
        pieces = [piece]
        for step in lay.high:
            pieces += [self.swap(p, step) for p in pieces]
        shape = (len(pieces), lay.half_rows, piece.shape[1])
        halves = call(functools.partial(merge_kernel, lay), name, pieces, [(shape, BF)] * 2, smem=0)
        parts = []
        for order, held in zip(self.orders, halves):
            near = self.swap(held, order[-2])
            parts += [held, near, self.swap(held, order[-1]), self.swap(near, order[-1])]
        return parts

    def grad_shapes(self, columns):
        lay = self.lay
        if lay.aligned:
            return [((lay.img_count, lay.half_rows, columns), BF)] * 4
        return [((2,) + lay.tiles + (columns,), BF)]

    def scatter_rows(self, parts):
        lay = self.lay
        if not lay.aligned:
            pieces = parts[0].reshape(2, lay.img_count, lay.rows, parts[0].shape[3])
            parts = []
            for part, order in enumerate(self.orders):
                mine = pieces[:, :, part * lay.half_rows : (part + 1) * lay.half_rows]
                mine = jnp.take(mine.reshape((-1,) + mine.shape[2:]), self.sources(order), axis=0)
                parts += [mine[: lay.img_count], mine[lay.img_count :]]
        sums = []
        for part, order in enumerate(self.orders):
            keep, send = parts[2 * part : 2 * part + 2]
            held = (keep.astype(F32) + self.swap(send, order[-1]).astype(F32)).astype(BF)
            half = lay.img_count // 2
            sums.append((held[:half].astype(F32) + self.swap(held[half:], order[-2]).astype(F32)).astype(BF))
        return self.scatter(jnp.concatenate(sums, 1), lay.high)


NAMES = ("qkv_bias", "proj_bias", "attn_gain", "attn_shift", "mlp_gain", "mlp_shift", "up_bias", "down_bias", "freqs")


def plan_vectors(lay):
    width, third, pairs = lay.width, lay.third, lay.head // 2
    devices = lay.img_count * 4
    heads = np.arange(HEADS).reshape(2, 2, HEADS // 4)

    def by_core(count, shape):
        return [np.take(np.arange(count).reshape(shape), core, len(shape) - 2).reshape(-1) for core in range(2)]

    plain = [np.arange(width)] * 2
    up = by_core(4 * width, (2, 2, width))
    freqs = []
    for core in range(2):
        pick = np.arange(width).reshape(2, HEADS, pairs)[:, heads[:, core].reshape(-1)]
        freqs.append(np.stack([pick, pick], 2).reshape(-1))
    qkv, qk, v = (by_core(n * width, (n, 2, 2, third)) for n in (3, 2, 1))

    def lay_out(members):
        plan, tables, start, offset = [], [[], [], [], []], 0, 0
        for pick, count in members:
            count //= devices
            plan.append((start, pick[0].size, offset, count))
            for core in range(2):
                tables[2 * core].append(pick[core] // count)
                tables[2 * core + 1].append(pick[core] % count)
            start += pick[0].size
            offset += count
        return plan, jnp.asarray(np.stack([np.concatenate(t) for t in tables]).astype(np.int32))

    rest = [(plain, width)] * 5 + [(up, 4 * width), (plain, width), (freqs, width)]
    given = lay_out([(qkv, 3 * width)] + rest)
    lay.at = {name: slice(p[0], p[0] + p[1]) for name, p in zip(NAMES, given[0])}
    return given, lay_out([(qk, 2 * width), (v, width)] + rest)


def make_body(img_count):
    def body(
        tokens, keep_mask, cotangent, qkv_weight, qkv_bias, proj_weight, proj_bias, attn_gain, attn_shift,
        mlp_gain, mlp_shift, up_weight, up_bias, down_weight, down_bias, rope_freqs,
    ):
        lay = Layout(img_count, tokens, qkv_weight.shape[0])
        me = Slice(lay)
        y, c, facts = me.y, me.c, me.facts
        images, band, width, length = lay.images, lay.band, lay.width, lay.length
        heads = HEADS // 2
        own, third = lay.own, lay.third
        half = length // 2
        block = proj_weight.shape[1]
        hidden = up_weight.shape[1]
        devices = img_count * 4
        vectors = (qkv_bias, proj_bias, attn_gain, attn_shift, mlp_gain, mlp_shift, up_bias, down_bias, rope_freqs)
        (plan, table), (grad_plan, grad_table) = plan_vectors(lay)

        def pick(flag, zero, one):
            return jnp.where(flag == 0, zero, one)

        def kernel(function, name, inputs, outs, scratch=(), **options):
            return call(functools.partial(function, lay), name, inputs, outs, scratch, **options)

        pack_rows = 2 * band + 16
        mine, other, third_send, first_piece, second_piece = kernel(
            pack_kernel, "pack",
            [facts, tokens.reshape(images, band, width), cotangent.reshape(images, band, width), keep_mask, qkv_weight, proj_weight,
             up_weight, down_weight.T, *[v.reshape(1, -1) for v in vectors]],
            [((pack_rows, width), BF), ((pack_rows, width), BF), ((lay.rows, 2 * 128), BF), ((lay.rows, 2 * third + block), BF),
             ((lay.rows, 2 * hidden), BF)], limit=12,
        )
        third_came = me.swap(third_send, "c")
        near = me.swap(other, "y")
        bands = [mine, near, me.swap(mine, "c"), me.swap(near, "c")]
        (first_piece,) = kernel(fit_kernel, "fit", [facts, third_came, first_piece], [((lay.rows, 3 * third + block), BF)])
        first = me.gather_rows(first_piece, "merge_first")
        second = me.gather_rows(second_piece, "merge_second")
        held = jnp.concatenate([b[2 * band + 1 : 2 * band + 2] for b in bands], 0)[None]
        vec_order = lay.high + [0]
        for step in vec_order:
            held = jnp.concatenate([held, me.swap(held, step)], 0)
        (vec,) = call(
            functools.partial(unpack_kernel, lay, plan), "unpack", [facts, held.reshape(devices, width), table],
            [((1, table.shape[1]), F32)], limit=24,
        )

        n_w = len(first)
        n_g = len(me.grad_shapes(1))
        a1, q, k, v, w_qkv, p_cols, cos, sin, kp, mask_bias = call(
            functools.partial(project_kernel, lay, n_w), "qkv", [facts, *bands, *first, vec],
            [((length, width), BF), ((length, own), BF), ((length, own), BF), ((length, own), BF), ((2, width, 3 * third), BF),
             ((width, 2 * block), BF), ((length, own), F32), ((length, own), F32), ((length, 1), F32), ((1, length), F32)],
            [((2,) + lay.tiles + (3 * third + block,), BF)], limit=24, us=5,
        )
        p_other = me.swap(p_cols, "c")
        ob, p = call(
            functools.partial(attend_kernel, lay, band), "attend", [q, k, v, mask_bias],
            [((length, own), BF), ((heads, length, length), BF)], smem=0, limit=12, us=11,
        )
        ob_other = me.swap(ob, "c")
        x1, a2, w_proj = call(
            functools.partial(middle_kernel, lay), "middle", [facts, *bands, ob, ob_other, p_cols, p_other, vec],
            [((length, width), F32), ((length, width), BF), ((width, width), BF)], limit=16, us=3,
        )
        part, m_send, dn, dn_send, d_up_bias, d_down_bias, *second_grads = call(
            functools.partial(mlp_kernel, lay, n_w, n_g, 256), "mlp", [facts, *bands, kp, x1, a2, *second, vec],
            [((half, width), F32), ((half, width), BF), ((length, width), F32), ((length, width), BF), ((1, 2 * hidden), F32),
             ((1, width), F32), *me.grad_shapes(2 * hidden)],
            [((length, width), BF), ((width, length), BF), ((width, length), BF), ((length, width), F32),
             (lay.tiles + (2 * hidden,), BF), (lay.tiles + (256,), BF)], limit=32, us=24,
        )
        d_second = me.scatter_rows(second_grads)
        dn_came = me.swap(dn_send, "c")
        m_came = me.swap(m_send, "c")
        out_half = (kp[:half] * (part + m_came.astype(F32))).astype(BF)
        dx_half, d_proj_bias, d_g2, d_s2, d_qk_bias, d_v_bias, d_freqs, dqkv, *first_grads = call(
            functools.partial(back_kernel, lay, n_g, band), "back",
            [facts, *bands, kp, x1, dn, dn_came, vec, w_proj, ob, ob_other, q, k, v, p, cos, sin, a1],
            [((half, width), F32), ((1, width), F32), ((1, width), F32), ((1, width), F32), ((1, 2 * own), F32), ((1, own), F32),
             ((1, 2 * own), F32), ((length, 3 * own), BF), *me.grad_shapes(3 * third + block)],
            [((length, width), BF), ((length, own), BF), ((length, own), F32), ((length, own), F32), ((length, own), F32),
             (lay.tiles + (3 * third + block,), BF)], limit=32, us=24,
        )
        d_first = me.scatter_rows(first_grads)
        dn1_keep, dn1_send = call(
            functools.partial(last_kernel, lay), "last", [dqkv, w_qkv], [((half, width), F32), ((half, width), BF)], smem=0, us=2
        )
        dn1_came = me.swap(dn1_send, "c")
        tg_keep, tg_send, d_g1, d_s1 = call(
            functools.partial(finish_kernel, lay), "finish", [bands[0], bands[1], dn1_keep, dn1_came, dx_half, vec],
            [((band, width), BF), ((band, width), BF), ((1, width), F32), ((1, width), F32)], smem=0,
        )

        grads = [d_qk_bias, d_v_bias, d_proj_bias, d_g1, d_s1, d_g2, d_s2, d_up_bias, d_down_bias, d_freqs]
        sums = call(
            functools.partial(repack_kernel, lay, grad_plan), "repack", [facts, grad_table, *grads], [((devices, 384), F32)],
            limit=24,
        )[0].reshape(img_count, 4, 384)
        for step in reversed(vec_order):
            count = sums.shape[0] // 2
            sums = sums[:count] + me.swap(sums[count:], step)
        sums = sums[0]
        sums = sums[:2] + me.swap(sums[2:], "c")
        total = sums[0] + me.swap(sums[1], "y")
        r = [total[offset : offset + count] for _, _, offset, count in grad_plan]

        def to_images(keep, send):
            came = me.swap(send, "y")
            return pick(y, jnp.stack([keep, came]), jnp.stack([came, keep])).reshape(tokens.shape)

        layer_out = to_images(out_half[:band], out_half[band:])
        tokens_grad = to_images(tg_keep, tg_send)

        d_up = d_second[:, :hidden].astype(F32)
        d_down = d_second[:, hidden:].T.astype(F32)
        d0, d1, d2 = d_first[:, :third], d_first[:, third : 2 * third], d_first[:, 2 * third : 3 * third]
        came = me.swap(pick(c, d2, d0), "c")
        d_qkv = pick(c, jnp.concatenate([d0, came, d1], 1), jnp.concatenate([d1, came, d2], 1)).astype(F32)
        d_proj = d_first[:, 3 * third :].astype(F32)
        return (
            layer_out, tokens_grad, d_qkv, r[0], r[1], d_proj, r[2], r[3], r[4], r[5], r[6], d_up, r[7], d_down, r[8], r[9],
        )

    return body


def solution(mesh):
    split = P(("img", "row"))
    both = P("img", "row")
    field = P("img", "row", None, None)
    return jax.shard_map(
        make_body(mesh.shape["img"]),
        mesh=mesh,
        in_specs=(
            field, P("img", "row", None), field, both, split, both, split, split, split, split, split, both, split,
            P("row", "img"), split, split,
        ),
        out_specs=(
            field, field, both, split, split, both, split, split, split, split, split, both, split, P("row", "img"),
            split, split,
        ),
        check_vma=False,
    )
```

profile of v0, /device:TPU:0, one launch (start us, length us, event | category | flops | bytes accessed | tf_op | source)
XLA Modules:
  0.0 283.4 jit_solution(10189453918249696242)
XLA Ops:
  13.8 3.0 %collective-permute-start = (bf16[304,768]{1,0:T(8,128)(2,1)S(1)}, bf16[304,768]{1,0:T(8,128)(2,1)S(1)}, u32[]{:S(2)}, u32[]{:S(2)}) collective-permute-start(bf16[304,768]{1,0:T(8,128)(2,1)S(1)} %get-tuple-element.69), channel_id=1, source_target_pairs={{0,2},{1,3},{2,0},{3,1},{4,6},{5,7},{6,4},{7,5},{8,10},{9,11},{10,... | collective-permute-start | bytes 1400840 | tf_op jit(solution)/shard_map/ppermute | solution.py:484
  17.4 2.6 collective-permute-start.18
  20.0 7.6 %collective-permute-done.t1 = bf16[304,768]{1,0:T(8,128)(2,1)S(1)} collective-permute-done((bf16[304,768]{1,0:T(8,128)(2,1)S(1)}, bf16[304,768]{1,0:T(8,128)(2,1)S(1)}, u32[]{:S(2)}, u32[]{:S(2)}) %collective-permute-start) | collective-permute-done | bytes 466976 | tf_op jit(solution)/shard_map/ppermute | solution.py:484
  28.2 2.9 %collective-permute-start.4 = (bf16[96,768]{1,0:T(8,128)(2,1)S(1)}, bf16[96,768]{1,0:T(8,128)(2,1)S(1)}, u32[]{:S(2)}, u32[]{:S(2)}) collective-permute-start(bf16[96,768]{1,0:T(8,128)(2,1)S(1)} %fit.1.refs_0_), channel_id=1, source_target_pairs={{0,16},{4,20},{8,24},{12,28},{16,0},{20,4},{24,8},{28,12},{1,17},{... | collective-permute-start | bytes 442376 | tf_op jit(solution)/shard_map/ppermute | solution.py:485
  31.1 1.6 collective-permute-start.5
  32.7 7.3 %collective-permute-done.4.refs_1_ = bf16[96,768]{1,0:T(8,128)(2,1)S(1)} collective-permute-done((bf16[96,768]{1,0:T(8,128)(2,1)S(1)}, bf16[96,768]{1,0:T(8,128)(2,1)S(1)}, u32[]{:S(2)}, u32[]{:S(2)}) %collective-permute-start.4) | collective-permute-done | bytes 147488 | tf_op jit(solution)/shard_map/ppermute | solution.py:485
  40.5 1.6 collective-permute-start.19
  42.6 4.1 %collective-permute-done.6.refs_3_ = bf16[96,768]{1,0:T(8,128)(2,1)S(1)} collective-permute-done((bf16[96,768]{1,0:T(8,128)(2,1)S(1)}, bf16[96,768]{1,0:T(8,128)(2,1)S(1)}, u32[]{:S(2)}, u32[]{:S(2)}) %collective-permute-start.6) | collective-permute-done | bytes 147488 | tf_op jit(solution)/shard_map/ppermute | solution.py:485
  48.1 1.6 collective-permute-start.7
  49.7 1.9 collective-permute-start.13
  51.6 5.0 %collective-permute-done.13 = bf16[1,4,768]{2,1,0:T(4,128)(2,1)S(1)} collective-permute-done((bf16[1,4,768]{2,1,0:T(4,128)(2,1)S(1)}, bf16[1,4,768]{2,1,0:T(4,128)(2,1)S(1)}, u32[]{:S(2)}, u32[]{:S(2)}) %collective-permute-start.13) | collective-permute-done | bytes 6176 | tf_op jit(solution)/shard_map/ppermute | solution.py:485
  56.6 4.2 %collective-permute-start.14 = (bf16[2,4,768]{2,1,0:T(4,128)(2,1)S(1)}, bf16[2,4,768]{2,1,0:T(4,128)(2,1)S(1)}, u32[]{:S(2)}, u32[]{:S(2)}) collective-permute-start(bf16[2,4,768]{2,1,0:T(4,128)(2,1)S(1)} %pad_maximum_fusion.6), channel_id=1, source_target_pairs={{0,8},{4,12},{8,0},{12,4},{16,24},{20,28},{24,16},{28,20},{1,9},{5... | collective-permute-start | bytes 36872 | tf_op jit(solution)/shard_map/ppermute | solution.py:485
  60.8 1.7 collective-permute-done.14
  62.4 1.5 collective-permute-start.11
  66.6 1.5 collective-permute-start.15
  68.2 8.5 %collective-permute-done.15 = bf16[4,4,768]{2,1,0:T(4,128)(2,1)S(1)} collective-permute-done((bf16[4,4,768]{2,1,0:T(4,128)(2,1)S(1)}, bf16[4,4,768]{2,1,0:T(4,128)(2,1)S(1)}, u32[]{:S(2)}, u32[]{:S(2)}) %collective-permute-start.15) | collective-permute-done | bytes 24608 | tf_op jit(solution)/shard_map/ppermute | solution.py:485
  76.7 1.5 collective-permute-start.21
  80.0 4.7 %qkv.1 = (bf16[576,768]{1,0:T(8,128)(2,1)S(1)}, bf16[576,384]{1,0:T(8,128)(2,1)S(1)}, bf16[576,384]{1,0:T(8,128)(2,1)S(1)}, bf16[576,384]{1,0:T(8,128)(2,1)S(1)}...) custom-call(s32[4]{0:T(128)S(1)} %pad_add_fusion.me_ref, ...), custom_call_target="tpu_custom_call" | custom-call | flops 5000000000 | bytes 1024 | tf_op jit(solution)/shard_map/qkv/pallas_call | solution.py:458
  84.7 10.5 %attend.1 = (bf16[576,384]{1,0:T(8,128)(2,1)S(1)}, bf16[6,576,576]{2,1,0:T(8,128)(2,1)S(1)}) custom-call(bf16[576,384]{1,0:T(8,128)(2,1)S(1)} %get-tuple-element.75.q_ref, bf16[576,384]{1,0:T(8,128)(2,1)S(1)} %get-tuple-element.76.k_ref, bf16[576,384]{1,0:T(8,128)(2,1)S(1)} %get-tuple-element.77.v_ref, f32[1,576]{1,0:T(1,128)S(1)} %get-tuple-element.78.bias_ref), custom_call_target="tpu_custom_call" | custom-call | flops 11000000512 | bytes 1024 | tf_op jit(solution)/shard_map/attend/pallas_call | solution.py:458
  95.2 2.1 copy-done.54
  100.4 1.5 collective-permute-start.26
  101.9 2.6 middle.1
  104.6 9.4 %collective-permute-done.22.refs_2_ = bf16[4,48,1536]{2,1,0:T(8,128)(2,1)S(1)} collective-permute-done((bf16[4,48,1536]{2,1,0:T(8,128)(2,1)S(1)}, bf16[4,48,1536]{2,1,0:T(8,128)(2,1)S(1)}, u32[]{:S(2)}, u32[]{:S(2)}) %collective-permute-start.22) | collective-permute-done | bytes 589856 | tf_op jit(solution)/shard_map/ppermute | solution.py:484
  114.0 1.5 collective-permute-done.25.refs_6_
  115.5 10.2 %collective-permute-done.23.refs_3_ = bf16[4,48,1536]{2,1,0:T(8,128)(2,1)S(1)} collective-permute-done((bf16[4,48,1536]{2,1,0:T(8,128)(2,1)}, bf16[4,48,1536]{2,1,0:T(8,128)(2,1)S(1)}, u32[]{:S(2)}, u32[]{:S(2)}) %collective-permute-start.23) | collective-permute-done | bytes 589856 | tf_op jit(solution)/shard_map/ppermute | solution.py:484
  130.9 14.9 %mlp.1 = (f32[288,768]{1,0:T(8,128)S(1)}, bf16[288,768]{1,0:T(8,128)(2,1)S(1)}, f32[576,768]{1,0:T(8,128)S(1)}, bf16[576,768]{1,0:T(8,128)(2,1)S(1)}, f32[1,1536...) custom-call(s32[4]{0:T(128)S(1)} %pad_add_fusion.me_ref, ...), custom_call_target="tpu_custom_call" | custom-call | flops 24000000000 | bytes 1024 | tf_op jit(solution)/shard_map/mlp/pallas_call | solution.py:458
  146.0 2.4 collective-permute-done.29.came_ref
  149.6 2.3 copy-done.55
  151.8 19.9 %back.1 = (f32[288,768]{1,0:T(8,128)S(1)}, f32[1,768]{1,0:T(1,128)S(1)}, f32[1,768]{1,0:T(1,128)S(1)}, f32[1,768]{1,0:T(1,128)S(1)}, f32[1,768]{1,0:T(1,128)S(1)...) custom-call(s32[4]{0:T(128)S(1)} %pad_add_fusion.me_ref, ...), custom_call_target="tpu_custom_call" | custom-call | flops 24000000000 | bytes 1024 | tf_op jit(solution)/shard_map/back/pallas_call | solution.py:458
  171.9 2.3 last.1
  182.8 1.8 finish.1
  186.3 1.5 collective-permute-start.39
  187.9 1.9 multiply_convert_fusion
  189.8 15.7 %collective-permute-done.39 = f32[4,4,384]{2,1,0:T(4,128)S(1)} collective-permute-done((f32[4,4,384]{2,1,0:T(4,128)S(1)}, f32[4,4,384]{2,1,0:T(4,128)S(1)}, u32[]{:S(2)}, u32[]{:S(2)}) %collective-permute-start.39) | collective-permute-done | bytes 24608 | tf_op jit(solution)/shard_map/ppermute | solution.py:485
  205.6 1.9 collective-permute-start.40
  208.5 1.5 collective-permute-start.28
  210.4 4.3 %collective-permute-done.28 = bf16[144,768]{1,0:T(8,128)(2,1)S(1)} collective-permute-done((bf16[144,768]{1,0:T(8,128)(2,1)S(1)}, bf16[144,768]{1,0:T(8,128)(2,1)S(1)}, u32[]{:S(2)}, u32[]{:S(2)}) %collective-permute-start.28) | collective-permute-done | bytes 221216 | tf_op jit(solution)/shard_map/ppermute | solution.py:484
  217.6 1.6 add_convert_fusion.1
  219.3 1.6 collective-permute-start.45
  221.5 7.2 %collective-permute-done.32 = bf16[8,48,768]{2,1,0:T(8,128)(2,1)S(1)} collective-permute-done((bf16[8,48,768]{2,1,0:T(8,128)(2,1)S(1)}, bf16[8,48,768]{2,1,0:T(8,128)(2,1)S(1)}, u32[]{:S(2)}, u32[]{:S(2)}) %collective-permute-start.32) | collective-permute-done | bytes 589856 | tf_op jit(solution)/shard_map/ppermute | solution.py:484
  229.4 3.9 %collective-permute-done.34 = bf16[8,48,768]{2,1,0:T(8,128)(2,1)S(1)} collective-permute-done((bf16[8,48,768]{2,1,0:T(8,128)(2,1)S(1)}, bf16[8,48,768]{2,1,0:T(8,128)(2,1)S(1)}, u32[]{:S(2)}, u32[]{:S(2)}) %collective-permute-start.34) | collective-permute-done | bytes 589856 | tf_op jit(solution)/shard_map/ppermute | solution.py:485
  234.1 1.6 add_convert_fusion
  235.7 1.5 collective-permute-start.47
  239.2 9.6 %collective-permute-done.33 = bf16[4,48,768]{2,1,0:T(8,128)(2,1)S(1)} collective-permute-done((bf16[4,48,768]{2,1,0:T(8,128)(2,1)S(1)}, bf16[4,48,768]{2,1,0:T(8,128)(2,1)S(1)}, u32[]{:S(2)}, u32[]{:S(2)}) %collective-permute-start.33) | collective-permute-done | bytes 294944 | tf_op jit(solution)/shard_map/ppermute | solution.py:485
  251.5 9.1 %collective-permute-done.36 = bf16[2,96,768]{2,1,0:T(8,128)(2,1)S(1)} collective-permute-done((bf16[2,96,768]{2,1,0:T(8,128)(2,1)S(1)}, bf16[2,96,768]{2,1,0:T(8,128)(2,1)S(1)}, u32[]{:S(2)}, u32[]{:S(2)}) %collective-permute-start.36) | collective-permute-done | bytes 294944 | tf_op jit(solution)/shard_map/ppermute | solution.py:485
  261.4 7.7 %collective-permute-done.37 = bf16[1,96,768]{2,1,0:T(8,128)(2,1)S(1)} collective-permute-done((bf16[1,96,768]{2,1,0:T(8,128)(2,1)S(1)}, bf16[1,96,768]{2,1,0:T(8,128)(2,1)S(1)}, u32[]{:S(2)}, u32[]{:S(2)}) %collective-permute-start.37) | collective-permute-done | bytes 147488 | tf_op jit(solution)/shard_map/ppermute | solution.py:485
  270.7 2.1 collective-permute-start.49
  275.6 6.9 %collective-permute-done.49 = bf16[1,96,1536]{2,1,0:T(8,128)(2,1)S(1)} collective-permute-done((bf16[1,96,1536]{2,1,0:T(8,128)(2,1)S(1)}, bf16[1,96,1536]{2,1,0:T(8,128)(2,1)S(1)}, u32[]{:S(2)}, u32[]{:S(2)}) %collective-permute-start.49) | collective-permute-done | bytes 294944 | tf_op jit(solution)/shard_map/ppermute | solution.py:485
  (255 shorter events, 58.4 us)
Async XLA Ops:
  13.8 13.7 %collective-permute-start = (bf16[304,768]{1,0:T(8,128)(2,1)S(1)}, bf16[304,768]{1,0:T(8,128)(2,1)S(1)}, u32[]{:S(2)}, u32[]{:S(2)}) collective-permute-start(bf16[304,768]{1,0:T(8,128)(2,1)S(1)} %get-tuple-element.69), channel_id=1, source_target_pairs={{0,2},{1,3},{2,0},{3,1},{4,6},{5,7},{6,4},{7,5},{8,10},{9,11},{10,... | collective-permute-start | bytes 1400840 | tf_op jit(solution)/shard_map/ppermute | solution.py:484
  16.9 10.7 %collective-permute-start.3 = (bf16[96,256]{1,0:T(8,128)(2,1)S(1)}, bf16[96,256]{1,0:T(8,128)(2,1)S(1)}, u32[]{:S(2)}, u32[]{:S(2)}) collective-permute-start(bf16[96,256]{1,0:T(8,128)(2,1)S(1)} %get-tuple-element.70), channel_id=1, source_target_pairs={{0,1},{1,0},{2,3},{3,2},{4,5},{5,4},{6,7},{7,6},{8,9},{9,8},{10,11... | collective-permute-start | bytes 147464 | tf_op jit(solution)/shard_map/ppermute | solution.py:482
  16.9 31.2 %collective-permute-start.1 = (bf16[304,768]{1,0:T(8,128)(2,1)S(1)}, bf16[304,768]{1,0:T(8,128)(2,1)S(1)}, u32[]{:S(2)}, u32[]{:S(2)}) collective-permute-start(bf16[304,768]{1,0:T(8,128)(2,1)S(1)} %get-tuple-element.68.t0), channel_id=1, source_target_pairs={{0,1},{1,0},{2,3},{3,2},{4,5},{5,4},{6,7},{7,6},{8,9},{9,8},{10,11... | collective-permute-start | bytes 1400840 | tf_op jit(solution)/shard_map/ppermute | solution.py:482
  17.4 24.7 %collective-permute-start.18 = (bf16[96,1536]{1,0:T(8,128)(2,1)S(1)}, bf16[96,1536]{1,0:T(8,128)(2,1)S(1)}, u32[]{:S(2)}, u32[]{:S(2)}) collective-permute-start(bf16[96,1536]{1,0:T(8,128)(2,1)S(1)} %get-tuple-element.83.refs_0_), channel_id=1, source_target_pairs={{0,16},{4,20},{8,24},{12,28},{16,0},{20,4},{24,8},{28,12},{1,17},{... | collective-permute-start | bytes 884744 | tf_op jit(solution)/shard_map/ppermute | solution.py:485
  27.6 22.1 %collective-permute-start.2 = (bf16[304,768]{1,0:T(8,128)(2,1)S(1)}, bf16[304,768]{1,0:T(8,128)(2,1)S(1)}, u32[]{:S(2)}, u32[]{:S(2)}) collective-permute-start(bf16[304,768]{1,0:T(8,128)(2,1)S(1)} %collective-permute-done.t1), channel_id=1, source_target_pairs={{0,1},{1,0},{2,3},{3,2},{4,5},{5,4},{6,7},{7,6},{8,9},{9,8},{10,11... | collective-permute-start | bytes 1400840 | tf_op jit(solution)/shard_map/ppermute | solution.py:482
  28.2 11.7 %collective-permute-start.4 = (bf16[96,768]{1,0:T(8,128)(2,1)S(1)}, bf16[96,768]{1,0:T(8,128)(2,1)S(1)}, u32[]{:S(2)}, u32[]{:S(2)}) collective-permute-start(bf16[96,768]{1,0:T(8,128)(2,1)S(1)} %fit.1.refs_0_), channel_id=1, source_target_pairs={{0,16},{4,20},{8,24},{12,28},{16,0},{20,4},{24,8},{28,12},{1,17},{... | collective-permute-start | bytes 442376 | tf_op jit(solution)/shard_map/ppermute | solution.py:485
  31.1 9.4 %collective-permute-start.5 = (bf16[96,768]{1,0:T(8,128)(2,1)S(1)}, bf16[96,768]{1,0:T(8,128)(2,1)S(1)}, u32[]{:S(2)}, u32[]{:S(2)}) collective-permute-start(bf16[96,768]{1,0:T(8,128)(2,1)S(1)} %fit.1.refs_0_), channel_id=1, source_target_pairs={{0,8},{4,12},{8,0},{12,4},{16,24},{20,28},{24,16},{28,20},{1,9},{5... | collective-permute-start | bytes 442376 | tf_op jit(solution)/shard_map/ppermute | solution.py:485
  39.9 6.8 %collective-permute-start.6 = (bf16[96,768]{1,0:T(8,128)(2,1)S(1)}, bf16[96,768]{1,0:T(8,128)(2,1)S(1)}, u32[]{:S(2)}, u32[]{:S(2)}) collective-permute-start(bf16[96,768]{1,0:T(8,128)(2,1)S(1)} %collective-permute-done.4.refs_1_), channel_id=1, source_target_pairs={{0,8},{4,12},{8,0},{12,4},{16,24},{20,28},{24,16},{28,20},{1,9},{5... | collective-permute-start | bytes 442376 | tf_op jit(solution)/shard_map/ppermute | solution.py:485
  40.5 23.5 %collective-permute-start.19 = (bf16[96,1536]{1,0:T(8,128)(2,1)S(1)}, bf16[96,1536]{1,0:T(8,128)(2,1)S(1)}, u32[]{:S(2)}, u32[]{:S(2)}) collective-permute-start(bf16[96,1536]{1,0:T(8,128)(2,1)S(1)} %get-tuple-element.83.refs_0_), channel_id=1, source_target_pairs={{0,8},{4,12},{8,0},{12,4},{16,24},{20,28},{24,16},{28,20},{1,9},{5... | collective-permute-start | bytes 884744 | tf_op jit(solution)/shard_map/ppermute | solution.py:485
  42.1 24.5 %collective-permute-start.20 = (bf16[96,1536]{1,0:T(8,128)(2,1)S(1)}, bf16[96,1536]{1,0:T(8,128)(2,1)S(1)}, u32[]{:S(2)}, u32[]{:S(2)}) collective-permute-start(bf16[96,1536]{1,0:T(8,128)(2,1)S(1)} %collective-permute-done.18.refs_1_), channel_id=1, source_target_pairs={{0,8},{4,12},{8,0},{12,4},{16,24},{20,28},{24,16},{28,20},{1,9},{5... | collective-permute-start | bytes 884744 | tf_op jit(solution)/shard_map/ppermute | solution.py:485
  47.6 17.0 %collective-permute-start.10 = (bf16[4,48,768]{2,1,0:T(8,128)(2,1)}, bf16[4,48,768]{2,1,0:T(8,128)(2,1)}, u32[]{:S(2)}, u32[]{:S(2)}) collective-permute-start(bf16[4,48,768]{2,1,0:T(8,128)(2,1)} %get-tuple-element.73.refs_4_), channel_id=1, source_target_pairs={{0,2},{1,3},{2,0},{3,1},{4,6},{5,7},{6,4},{7,5},{8,10},{9,11},{10,... | collective-permute-start | bytes 884744 | tf_op jit(solution)/shard_map/ppermute | solution.py:484
  48.1 17.1 %collective-permute-start.7 = (bf16[4,48,768]{2,1,0:T(8,128)(2,1)}, bf16[4,48,768]{2,1,0:T(8,128)(2,1)}, u32[]{:S(2)}, u32[]{:S(2)}) collective-permute-start(bf16[4,48,768]{2,1,0:T(8,128)(2,1)} %get-tuple-element.72.refs_0_), channel_id=1, source_target_pairs={{0,4},{4,0},{8,12},{12,8},{16,20},{20,16},{24,28},{28,24},{1,5},{5... | collective-permute-start | bytes 884744 | tf_op jit(solution)/shard_map/ppermute | solution.py:485
  49.7 6.9 %collective-permute-start.13 = (bf16[1,4,768]{2,1,0:T(4,128)(2,1)S(1)}, bf16[1,4,768]{2,1,0:T(4,128)(2,1)S(1)}, u32[]{:S(2)}, u32[]{:S(2)}) collective-permute-start(bf16[1,4,768]{2,1,0:T(4,128)(2,1)S(1)} %maximum_bitcast_fusion), channel_id=1, source_target_pairs={{0,16},{4,20},{8,24},{12,28},{16,0},{20,4},{24,8},{28,12},{1,17},{... | collective-permute-start | bytes 18440 | tf_op jit(solution)/shard_map/ppermute | solution.py:485
  56.6 5.9 %collective-permute-start.14 = (bf16[2,4,768]{2,1,0:T(4,128)(2,1)S(1)}, bf16[2,4,768]{2,1,0:T(4,128)(2,1)S(1)}, u32[]{:S(2)}, u32[]{:S(2)}) collective-permute-start(bf16[2,4,768]{2,1,0:T(4,128)(2,1)S(1)} %pad_maximum_fusion.6), channel_id=1, source_target_pairs={{0,8},{4,12},{8,0},{12,4},{16,24},{20,28},{24,16},{28,20},{1,9},{5... | collective-permute-start | bytes 36872 | tf_op jit(solution)/shard_map/ppermute | solution.py:485
  62.4 16.8 %collective-permute-start.11 = (bf16[4,48,768]{2,1,0:T(8,128)(2,1)}, bf16[4,48,768]{2,1,0:T(8,128)(2,1)}, u32[]{:S(2)}, u32[]{:S(2)}) collective-permute-start(bf16[4,48,768]{2,1,0:T(8,128)(2,1)} %get-tuple-element.73.refs_4_), channel_id=1, source_target_pairs={{0,4},{4,0},{8,12},{12,8},{16,20},{20,16},{24,28},{28,24},{1,5},{5... | collective-permute-start | bytes 884744 | tf_op jit(solution)/shard_map/ppermute | solution.py:485
  64.0 16.0 %collective-permute-start.8 = (bf16[4,48,768]{2,1,0:T(8,128)(2,1)}, bf16[4,48,768]{2,1,0:T(8,128)(2,1)}, u32[]{:S(2)}, u32[]{:S(2)}) collective-permute-start(bf16[4,48,768]{2,1,0:T(8,128)(2,1)} %get-tuple-element.72.refs_0_), channel_id=1, source_target_pairs={{0,2},{1,3},{2,0},{3,1},{4,6},{5,7},{6,4},{7,5},{8,10},{9,11},{10,... | collective-permute-start | bytes 884744 | tf_op jit(solution)/shard_map/ppermute | solution.py:484
  64.6 15.4 %collective-permute-start.12 = (bf16[4,48,768]{2,1,0:T(8,128)(2,1)}, bf16[4,48,768]{2,1,0:T(8,128)(2,1)}, u32[]{:S(2)}, u32[]{:S(2)}) collective-permute-start(bf16[4,48,768]{2,1,0:T(8,128)(2,1)} %collective-permute-done.10.refs_5_), channel_id=1, source_target_pairs={{0,4},{4,0},{8,12},{12,8},{16,20},{20,16},{24,28},{28,24},{1,5},{5... | collective-permute-start | bytes 884744 | tf_op jit(solution)/shard_map/ppermute | solution.py:485
  65.2 14.8 %collective-permute-start.9 = (bf16[4,48,768]{2,1,0:T(8,128)(2,1)}, bf16[4,48,768]{2,1,0:T(8,128)(2,1)}, u32[]{:S(2)}, u32[]{:S(2)}) collective-permute-start(bf16[4,48,768]{2,1,0:T(8,128)(2,1)} %collective-permute-done.7.refs_1_), channel_id=1, source_target_pairs={{0,2},{1,3},{2,0},{3,1},{4,6},{5,7},{6,4},{7,5},{8,10},{9,11},{10,... | collective-permute-start | bytes 884744 | tf_op jit(solution)/shard_map/ppermute | solution.py:484
  66.6 10.1 %collective-permute-start.15 = (bf16[4,4,768]{2,1,0:T(4,128)(2,1)S(1)}, bf16[4,4,768]{2,1,0:T(4,128)(2,1)S(1)}, u32[]{:S(2)}, u32[]{:S(2)}) collective-permute-start(bf16[4,4,768]{2,1,0:T(4,128)(2,1)S(1)} %pad_maximum_fusion.5), channel_id=1, source_target_pairs={{0,4},{4,0},{8,12},{12,8},{16,20},{20,16},{24,28},{28,24},{1,5},{5... | collective-permute-start | bytes 73736 | tf_op jit(solution)/shard_map/ppermute | solution.py:485
  76.7 22.4 %collective-permute-start.21 = (bf16[4,48,1536]{2,1,0:T(8,128)(2,1)S(1)}, bf16[4,48,1536]{2,1,0:T(8,128)(2,1)}, u32[]{:S(2)}, u32[]{:S(2)}) collective-permute-start(bf16[4,48,1536]{2,1,0:T(8,128)(2,1)S(1)} %get-tuple-element.84.refs_0_), channel_id=1, source_target_pairs={{0,4},{4,0},{8,12},{12,8},{16,20},{20,16},{24,28},{28,24},{1,5},{5... | collective-permute-start | bytes 1769480 | tf_op jit(solution)/shard_map/ppermute | solution.py:485
  79.3 20.5 %collective-permute-start.24 = (bf16[4,48,1536]{2,1,0:T(8,128)(2,1)S(1)}, bf16[4,48,1536]{2,1,0:T(8,128)(2,1)S(1)}, u32[]{:S(2)}, u32[]{:S(2)}) collective-permute-start(bf16[4,48,1536]{2,1,0:T(8,128)(2,1)S(1)} %get-tuple-element.85.refs_4_), channel_id=1, source_target_pairs={{0,2},{1,3},{2,0},{3,1},{4,6},{5,7},{6,4},{7,5},{8,10},{9,11},{10,... | collective-permute-start | bytes 1769480 | tf_op jit(solution)/shard_map/ppermute | solution.py:484
  97.2 3.2 %collective-permute-start.16 = (bf16[576,384]{1,0:T(8,128)(2,1)S(1)}, bf16[576,384]{1,0:T(8,128)(2,1)S(1)}, u32[]{:S(2)}, u32[]{:S(2)}) collective-permute-start(bf16[576,384]{1,0:T(8,128)(2,1)S(1)} %get-tuple-element.79.ob_ref), channel_id=1, source_target_pairs={{0,1},{1,0},{2,3},{3,2},{4,5},{5,4},{6,7},{7,6},{8,9},{9,8},{10,11... | collective-permute-start | bytes 1327112 | tf_op jit(solution)/shard_map/ppermute | solution.py:482
  97.3 4.6 %collective-permute-start.17 = (bf16[768,384]{1,0:T(8,128)(2,1)S(1)}, bf16[768,384]{1,0:T(8,128)(2,1)S(1)}, u32[]{:S(2)}, u32[]{:S(2)}) collective-permute-start(bf16[768,384]{1,0:T(8,128)(2,1)S(1)} %get-tuple-element.80.p_ref), channel_id=1, source_target_pairs={{0,1},{1,0},{2,3},{3,2},{4,5},{5,4},{6,7},{7,6},{8,9},{9,8},{10,11... | collective-permute-start | bytes 1769480 | tf_op jit(solution)/shard_map/ppermute | solution.py:482
  97.8 16.2 %collective-permute-start.22 = (bf16[4,48,1536]{2,1,0:T(8,128)(2,1)S(1)}, bf16[4,48,1536]{2,1,0:T(8,128)(2,1)S(1)}, u32[]{:S(2)}, u32[]{:S(2)}) collective-permute-start(bf16[4,48,1536]{2,1,0:T(8,128)(2,1)S(1)} %get-tuple-element.84.refs_0_), channel_id=1, source_target_pairs={{0,2},{1,3},{2,0},{3,1},{4,6},{5,7},{6,4},{7,5},{8,10},{9,11},{10,... | collective-permute-start | bytes 1769480 | tf_op jit(solution)/shard_map/ppermute | solution.py:484
  99.2 16.3 %collective-permute-start.25 = (bf16[4,48,1536]{2,1,0:T(8,128)(2,1)S(1)}, bf16[4,48,1536]{2,1,0:T(8,128)(2,1)S(1)}, u32[]{:S(2)}, u32[]{:S(2)}) collective-permute-start(bf16[4,48,1536]{2,1,0:T(8,128)(2,1)S(1)} %get-tuple-element.85.refs_4_), channel_id=1, source_target_pairs={{0,4},{4,0},{8,12},{12,8},{16,20},{20,16},{24,28},{28,24},{1,5},{5... | collective-permute-start | bytes 1769480 | tf_op jit(solution)/shard_map/ppermute | solution.py:485
  99.8 25.9 %collective-permute-start.23 = (bf16[4,48,1536]{2,1,0:T(8,128)(2,1)}, bf16[4,48,1536]{2,1,0:T(8,128)(2,1)S(1)}, u32[]{:S(2)}, u32[]{:S(2)}) collective-permute-start(bf16[4,48,1536]{2,1,0:T(8,128)(2,1)} %collective-permute-done.21.refs_1_), channel_id=1, source_target_pairs={{0,2},{1,3},{2,0},{3,1},{4,6},{5,7},{6,4},{7,5},{8,10},{9,11},{10,... | collective-permute-start | bytes 1769480 | tf_op jit(solution)/shard_map/ppermute | solution.py:484
  100.4 26.4 %collective-permute-start.26 = (bf16[4,48,1536]{2,1,0:T(8,128)(2,1)S(1)}, bf16[4,48,1536]{2,1,0:T(8,128)(2,1)S(1)}, u32[]{:S(2)}, u32[]{:S(2)}) collective-permute-start(bf16[4,48,1536]{2,1,0:T(8,128)(2,1)S(1)} %collective-permute-done.24.refs_5_), channel_id=1, source_target_pairs={{0,4},{4,0},{8,12},{12,8},{16,20},{20,16},{24,28},{28,24},{1,5},{5... | collective-permute-start | bytes 1769480 | tf_op jit(solution)/shard_map/ppermute | solution.py:485
  145.9 2.5 collective-permute-start.29
  175.4 12.5 %collective-permute-start.27 = (bf16[288,768]{1,0:T(8,128)(2,1)}, bf16[288,768]{1,0:T(8,128)(2,1)}, u32[]{:S(2)}, u32[]{:S(2)}) collective-permute-start(bf16[288,768]{1,0:T(8,128)(2,1)} %copy-done.26), channel_id=1, source_target_pairs={{0,1},{1,0},{2,3},{3,2},{4,5},{5,4},{6,7},{7,6},{8,9},{9,8},{10,11... | collective-permute-start | bytes 1327112 | tf_op jit(solution)/shard_map/ppermute | solution.py:482
  176.5 41.1 %collective-permute-start.44 = (bf16[8,48,1536]{2,1,0:T(8,128)(2,1)}, bf16[8,48,1536]{2,1,0:T(8,128)(2,1)}, u32[]{:S(2)}, u32[]{:S(2)}) collective-permute-start(bf16[8,48,1536]{2,1,0:T(8,128)(2,1)} %copy-done.15), channel_id=1, source_target_pairs={{0,2},{1,3},{2,0},{3,1},{4,6},{5,7},{6,4},{7,5},{8,10},{9,11},{10,... | collective-permute-start | bytes 3538952 | tf_op jit(solution)/shard_map/ppermute | solution.py:484
  177.1 57.0 %collective-permute-start.46 = (bf16[8,48,1536]{2,1,0:T(8,128)(2,1)}, bf16[8,48,1536]{2,1,0:T(8,128)(2,1)}, u32[]{:S(2)}, u32[]{:S(2)}) collective-permute-start(bf16[8,48,1536]{2,1,0:T(8,128)(2,1)} %copy-done.14), channel_id=1, source_target_pairs={{0,4},{4,0},{8,12},{12,8},{16,20},{20,16},{24,28},{28,24},{1,5},{5... | collective-permute-start | bytes 3538952 | tf_op jit(solution)/shard_map/ppermute | solution.py:485
  186.3 19.2 %collective-permute-start.39 = (f32[4,4,384]{2,1,0:T(4,128)S(1)}, f32[4,4,384]{2,1,0:T(4,128)S(1)}, u32[]{:S(2)}, u32[]{:S(2)}) collective-permute-start(f32[4,4,384]{2,1,0:T(4,128)S(1)} %slice.180), channel_id=1, source_target_pairs={{0,4},{4,0},{8,12},{12,8},{16,20},{20,16},{24,28},{28,24},{1,5},{5... | collective-permute-start | bytes 73736 | tf_op jit(solution)/shard_map/ppermute | solution.py:485
  205.6 4.5 %collective-permute-start.40 = (f32[2,4,384]{2,1,0:T(4,128)S(1)}, f32[2,4,384]{2,1,0:T(4,128)S(1)}, u32[]{:S(2)}, u32[]{:S(2)}) collective-permute-start(f32[2,4,384]{2,1,0:T(4,128)S(1)} %slice.231), channel_id=1, source_target_pairs={{0,8},{4,12},{8,0},{12,4},{16,24},{20,28},{24,16},{28,20},{1,9},{5... | collective-permute-start | bytes 36872 | tf_op jit(solution)/shard_map/ppermute | solution.py:485
  208.5 6.2 %collective-permute-start.28 = (bf16[144,768]{1,0:T(8,128)(2,1)S(1)}, bf16[144,768]{1,0:T(8,128)(2,1)S(1)}, u32[]{:S(2)}, u32[]{:S(2)}) collective-permute-start(bf16[144,768]{1,0:T(8,128)(2,1)S(1)} %get-tuple-element.123), channel_id=1, source_target_pairs={{0,2},{1,3},{2,0},{3,1},{4,6},{5,7},{6,4},{7,5},{8,10},{9,11},{10,... | collective-permute-start | bytes 663560 | tf_op jit(solution)/shard_map/ppermute | solution.py:484
  210.1 7.5 %collective-permute-start.41 = (f32[1,4,384]{2,1,0:T(4,128)S(1)}, f32[1,4,384]{2,1,0:T(4,128)S(1)}, u32[]{:S(2)}, u32[]{:S(2)}) collective-permute-start(f32[1,4,384]{2,1,0:T(4,128)S(1)} %slice.233), channel_id=1, source_target_pairs={{0,16},{4,20},{8,24},{12,28},{16,0},{20,4},{24,8},{28,12},{1,17},{... | collective-permute-start | bytes 18440 | tf_op jit(solution)/shard_map/ppermute | solution.py:485
  215.5 13.1 %collective-permute-start.32 = (bf16[8,48,768]{2,1,0:T(8,128)(2,1)S(1)}, bf16[8,48,768]{2,1,0:T(8,128)(2,1)S(1)}, u32[]{:S(2)}, u32[]{:S(2)}) collective-permute-start(bf16[8,48,768]{2,1,0:T(8,128)(2,1)S(1)} %copy-done.19), channel_id=1, source_target_pairs={{0,2},{1,3},{2,0},{3,1},{4,6},{5,7},{6,4},{7,5},{8,10},{9,11},{10,... | collective-permute-start | bytes 1769480 | tf_op jit(solution)/shard_map/ppermute | solution.py:484
  217.0 16.3 %collective-permute-start.34 = (bf16[8,48,768]{2,1,0:T(8,128)(2,1)S(1)}, bf16[8,48,768]{2,1,0:T(8,128)(2,1)S(1)}, u32[]{:S(2)}, u32[]{:S(2)}) collective-permute-start(bf16[8,48,768]{2,1,0:T(8,128)(2,1)S(1)} %copy-done.17), channel_id=1, source_target_pairs={{0,4},{4,0},{8,12},{12,8},{16,20},{20,16},{24,28},{28,24},{1,5},{5... | collective-permute-start | bytes 1769480 | tf_op jit(solution)/shard_map/ppermute | solution.py:485
  217.5 3.3 %collective-permute-start.42 = (f32[2,384]{1,0:T(2,128)S(1)}, f32[2,384]{1,0:T(2,128)S(1)}, u32[]{:S(2)}, u32[]{:S(2)}) collective-permute-start(f32[2,384]{1,0:T(2,128)S(1)} %slice_bitcast_fusion), channel_id=1, source_target_pairs={{0,1},{1,0},{2,3},{3,2},{4,5},{5,4},{6,7},{7,6},{8,9},{9,8},{10,11... | collective-permute-start | bytes 9224 | tf_op jit(solution)/shard_map/ppermute | solution.py:482
  219.3 30.2 %collective-permute-start.45 = (bf16[4,48,1536]{2,1,0:T(8,128)(2,1)S(1)}, bf16[4,48,1536]{2,1,0:T(8,128)(2,1)S(1)}, u32[]{:S(2)}, u32[]{:S(2)}) collective-permute-start(bf16[4,48,1536]{2,1,0:T(8,128)(2,1)S(1)} %slice.240), channel_id=1, source_target_pairs={{0,4},{4,0},{8,12},{12,8},{16,20},{20,16},{24,28},{28,24},{1,5},{5... | collective-permute-start | bytes 1769480 | tf_op jit(solution)/shard_map/ppermute | solution.py:485
  220.9 16.4 %collective-permute-start.43 = (f32[384]{0:T(512)S(1)}, f32[384]{0:T(512)S(1)}, u32[]{:S(2)}, u32[]{:S(2)}) collective-permute-start(f32[384]{0:T(512)S(1)} %get-tuple-element.120), channel_id=1, source_target_pairs={{0,2},{1,3},{2,0},{3,1},{4,6},{5,7},{6,4},{7,5},{8,10},{9,11},{10,... | collective-permute-start | bytes 4616 | tf_op jit(solution)/shard_map/ppermute | solution.py:484
  228.8 20.0 %collective-permute-start.33 = (bf16[4,48,768]{2,1,0:T(8,128)(2,1)S(1)}, bf16[4,48,768]{2,1,0:T(8,128)(2,1)S(1)}, u32[]{:S(2)}, u32[]{:S(2)}) collective-permute-start(bf16[4,48,768]{2,1,0:T(8,128)(2,1)S(1)} %slice.218), channel_id=1, source_target_pairs={{0,4},{4,0},{8,12},{12,8},{16,20},{20,16},{24,28},{28,24},{1,5},{5... | collective-permute-start | bytes 884744 | tf_op jit(solution)/shard_map/ppermute | solution.py:485
  233.5 15.4 %collective-permute-start.35 = (bf16[4,48,768]{2,1,0:T(8,128)(2,1)S(1)}, bf16[4,48,768]{2,1,0:T(8,128)(2,1)S(1)}, u32[]{:S(2)}, u32[]{:S(2)}) collective-permute-start(bf16[4,48,768]{2,1,0:T(8,128)(2,1)S(1)} %slice.220), channel_id=1, source_target_pairs={{0,2},{1,3},{2,0},{3,1},{4,6},{5,7},{6,4},{7,5},{8,10},{9,11},{10,... | collective-permute-start | bytes 884744 | tf_op jit(solution)/shard_map/ppermute | solution.py:484
  235.7 15.1 %collective-permute-start.47 = (bf16[4,48,1536]{2,1,0:T(8,128)(2,1)S(1)}, bf16[4,48,1536]{2,1,0:T(8,128)(2,1)S(1)}, u32[]{:S(2)}, u32[]{:S(2)}) collective-permute-start(bf16[4,48,1536]{2,1,0:T(8,128)(2,1)S(1)} %slice.242), channel_id=1, source_target_pairs={{0,2},{1,3},{2,0},{3,1},{4,6},{5,7},{6,4},{7,5},{8,10},{9,11},{10,... | collective-permute-start | bytes 1769480 | tf_op jit(solution)/shard_map/ppermute | solution.py:484
  237.3 36.3 %collective-permute-start.31 = (bf16[144,768]{1,0:T(8,128)(2,1)S(1)}, bf16[144,768]{1,0:T(8,128)(2,1)S(1)}, u32[]{:S(2)}, u32[]{:S(2)}) collective-permute-start(bf16[144,768]{1,0:T(8,128)(2,1)S(1)} %copy-done.31), channel_id=1, source_target_pairs={{0,2},{1,3},{2,0},{3,1},{4,6},{5,7},{6,4},{7,5},{8,10},{9,11},{10,... | collective-permute-start | bytes 663560 | tf_op jit(solution)/shard_map/ppermute | solution.py:484
  249.0 11.6 %collective-permute-start.36 = (bf16[2,96,768]{2,1,0:T(8,128)(2,1)S(1)}, bf16[2,96,768]{2,1,0:T(8,128)(2,1)S(1)}, u32[]{:S(2)}, u32[]{:S(2)}) collective-permute-start(bf16[2,96,768]{2,1,0:T(8,128)(2,1)S(1)} %pad_maximum_fusion.1), channel_id=1, source_target_pairs={{0,8},{4,12},{8,0},{12,4},{16,24},{20,28},{24,16},{28,20},{1,9},{5... | collective-permute-start | bytes 884744 | tf_op jit(solution)/shard_map/ppermute | solution.py:485
  251.0 19.5 %collective-permute-start.48 = (bf16[2,96,1536]{2,1,0:T(8,128)(2,1)S(1)}, bf16[2,96,1536]{2,1,0:T(8,128)(2,1)S(1)}, u32[]{:S(2)}, u32[]{:S(2)}) collective-permute-start(bf16[2,96,1536]{2,1,0:T(8,128)(2,1)S(1)} %pad_maximum_fusion), channel_id=1, source_target_pairs={{0,8},{4,12},{8,0},{12,4},{16,24},{20,28},{24,16},{28,20},{1,9},{5... | collective-permute-start | bytes 1769480 | tf_op jit(solution)/shard_map/ppermute | solution.py:485
  260.7 8.4 %collective-permute-start.37 = (bf16[1,96,768]{2,1,0:T(8,128)(2,1)S(1)}, bf16[1,96,768]{2,1,0:T(8,128)(2,1)S(1)}, u32[]{:S(2)}, u32[]{:S(2)}) collective-permute-start(bf16[1,96,768]{2,1,0:T(8,128)(2,1)S(1)} %slice.224), channel_id=1, source_target_pairs={{0,16},{4,20},{8,24},{12,28},{16,0},{20,4},{24,8},{28,12},{1,17},{... | collective-permute-start | bytes 442376 | tf_op jit(solution)/shard_map/ppermute | solution.py:485
  270.7 11.7 %collective-permute-start.49 = (bf16[1,96,1536]{2,1,0:T(8,128)(2,1)S(1)}, bf16[1,96,1536]{2,1,0:T(8,128)(2,1)S(1)}, u32[]{:S(2)}, u32[]{:S(2)}) collective-permute-start(bf16[1,96,1536]{2,1,0:T(8,128)(2,1)S(1)} %slice.246), channel_id=1, source_target_pairs={{0,16},{4,20},{8,24},{12,28},{16,0},{20,4},{24,8},{28,12},{1,17},{... | collective-permute-start | bytes 884744 | tf_op jit(solution)/shard_map/ppermute | solution.py:485
  (70 other events, 658.2 us)
where the time goes:
time: 285 us; the launch traced here: 283 us
  waiting for transfers between devices  126 us (44%)
  Pallas kernels  60.9 us (21%)
  starting transfers between devices  51.7 us (18%)
  local copies, waits for them, and re-layouts  32.6 us (11%)
  other arithmetic  10.4 us (4%)
    ppermute x26, waiting for transfers between devices, swap(): lax.ppermute(array, 'img', [(i, i ^ 1 << step) for i in range(self.lay.im...  83.6 us
    pallas_call x13, Pallas kernels, call(): pl.pallas_call(kernel, out_shape=[jax.ShapeDtypeStruct(shape, dtype) for...  60.9 us
    ppermute x14, waiting for transfers between devices, swap(): return lax.ppermute(array, 'row', [(r, r ^ 2) for r in range(4)])  39.8 us
    ppermute x26, starting transfers between devices, swap(): lax.ppermute(array, 'img', [(i, i ^ 1 << step) for i in range(self.lay.im...  34.6 us
    unnamed x137, local copies, waits for them, and re-layouts  28.8 us
    ppermute x14, starting transfers between devices, swap(): return lax.ppermute(array, 'row', [(r, r ^ 2) for r in range(4)])  15.5 us
  transfers between devices with their start and end apart: 50, of which 22 were waited for; matrix products, arithmetic and copies ran while one was open for 5% of the time, Pallas kernels for 8%

commit v1 on v0

--- a/solution.py
+++ b/solution.py
@@ -15,7 +15,8 @@
 F32 = jnp.float32
 MIB = 2**20
 VMEM = pl.BlockSpec(memory_space=pltpu.VMEM)
-SMEM = pl.BlockSpec(memory_space=pltpu.SMEM)
+HBM = pl.BlockSpec(memory_space=pltpu.MemorySpace.HBM)
+PACKED = 384
 
 
 def dot(left, right, dims):
@@ -48,6 +49,11 @@
 
 def column_sum(value):
     return jnp.sum(value, 0, keepdims=True)
+
+
+def here():
+    row = lax.axis_index("row")
+    return lax.axis_index("img"), row >> 1, row & 1, row
 
 
 class Layout:
@@ -74,26 +80,27 @@
         return (high + ((img_rel & 1) << top), y_rel), (high + (y_rel << top), img_rel & 1)
 
 
-def load_pieces(lay, me_ref, refs, y_rel, target):
+def load_pieces(lay, refs, y_rel, target):
     if not lay.aligned:
-        target[...] = refs[0][me_ref[1] ^ y_rel]
+        target[...] = refs[0][here()[1] ^ y_rel]
         return
     half = lay.half_rows
-    base = lay.img_count // 2
+    count = len(refs) // 2
     for img_rel in range(lay.img_count):
         for part, (slot, last) in enumerate(lay.slots(img_rel, y_rel)):
-            ref = refs[4 * part + 2 * last + slot // base]
-            target[img_rel ^ me_ref[0], part * half : (part + 1) * half] = ref[slot % base]
-
-
-def store_pieces(lay, me_ref, refs, y_rel, columns, source):
+            which, slot = divmod((slot + last * lay.img_count) * count, 2 * lay.img_count)
+            ref, slot = refs[part * count + which], slot // count
+            target[img_rel ^ here()[0], part * half : (part + 1) * half] = ref[slot, :half]
+
+
+def store_pieces(lay, refs, y_rel, columns, source):
     if not lay.aligned:
-        refs[0][me_ref[1] ^ y_rel, :, :, columns] = source[...]
+        refs[0][here()[1] ^ y_rel, :, :, columns] = source[...]
         return
     half = lay.half_rows
     for img_rel in range(lay.img_count):
         for part, (slot, last) in enumerate(lay.slots(img_rel, y_rel)):
-            refs[2 * part + last][slot, :, columns] = source[img_rel ^ me_ref[0], part * half : (part + 1) * half]
+            refs[2 * part + last][slot, :half, columns] = source[img_rel ^ here()[0], part * half : (part + 1) * half]
 
 
 def halves_of(lay, value):
@@ -104,35 +111,51 @@
     return jnp.where(first, pltpu.roll(value, width - pairs, 1), pltpu.roll(value, pairs, 1))
 
 
-def pack_kernel(lay, me_ref, tok_ref, cot_ref, mask_ref, qkv_ref, proj_ref, up_ref, down_ref, *refs):
-    vectors = refs[:9]
-    mine_ref, other_ref, third_ref, first_ref, second_ref = refs[9:]
-    y = me_ref[1]
-    band, third, width = lay.band, lay.third, lay.width
-    third_ref[:, :third] = qkv_ref[:, third : 2 * third].astype(BF)
-    third_ref[:, third:] = jnp.zeros((lay.rows, third_ref.shape[1] - third), BF)
-    first_ref[:, :third] = qkv_ref[:, :third].astype(BF)
-    first_ref[:, third : 2 * third] = qkv_ref[:, 2 * third :].astype(BF)
-    first_ref[:, 2 * third :] = proj_ref[...].astype(BF)
-    second_ref[:, :width] = up_ref[...].astype(BF)
-    second_ref[:, width:] = down_ref[...].astype(BF)
-    packed = jnp.concatenate([v[...] for v in vectors], 1)
-    packed = jnp.concatenate([packed, jnp.zeros((1, width - packed.shape[1]), F32)], 1)
+def pack_kernel(lay, *refs):
+    tok, cot, mask, qkv, proj, up, down, *vectors = refs[:16]
+    mine_ref, other_ref, third_ref, first_ref, second_ref = refs[16:21]
+    mask_in, qkv_in, proj_in, up_in, down_in, *vectors_in = refs[21:35]
+    sems = refs[35]
+    y = here()[1]
+    band, third, width, rows = lay.band, lay.third, lay.width, lay.rows
+    pairs = [(qkv, qkv_in), (proj, proj_in), *zip(vectors, vectors_in), (up, up_in), (down, down_in), (mask, mask_in)]
+    for ref, which in ((other_ref, 1 - y), (mine_ref, y)):
+        pairs += [(tok.at[which], ref.at[:band]), (cot.at[which], ref.at[band : 2 * band])]
+    copies = [pltpu.make_async_copy(source, target, sems.at[n]) for n, (source, target) in enumerate(pairs)]
+    for copy in copies:
+        copy.start()
+    for copy in copies[:11]:
+        copy.wait()
+    packed = jnp.concatenate([v[...] for v in vectors_in], 1)
+    packed = jnp.concatenate([packed, jnp.zeros((1, PACKED - packed.shape[1]), F32)], 1).astype(BF)
+    third_ref[:, :third] = qkv_in[:, third : 2 * third].astype(BF)
+    third_ref[:, third:] = jnp.zeros((rows, third_ref.shape[1] - third), BF)
+    third_ref[0:1, third_ref.shape[1] - PACKED :] = packed
+    first_ref[:rows, :third] = qkv_in[:, :third].astype(BF)
+    first_ref[:rows, third : 2 * third] = qkv_in[:, 2 * third :].astype(BF)
+    first_ref[:rows, 2 * third :] = proj_in[...].astype(BF)
+    first_ref[rows:] = jnp.zeros((16, first_ref.shape[1]), BF)
+    first_ref[rows : rows + 1, :PACKED] = packed
+    for copy in copies[11:]:
+        copy.wait()
+    second_ref[:, :width] = up_in[...].astype(BF)
+    second_ref[:, width:] = down_in[...].astype(BF)
     for ref, which in ((mine_ref, y), (other_ref, 1 - y)):
-        ref[:band] = tok_ref[which]
-        ref[band : 2 * band] = cot_ref[which]
-        keep = mask_ref[which].astype(F32)
+        keep = mask_in[which].astype(F32)
         flat = jnp.concatenate([keep[r : r + 1] for r in range(lay.band_rows)], 1)
         flat = jnp.concatenate([flat, jnp.zeros((1, width - band), F32)], 1)
-        ref[2 * band :] = jnp.concatenate([flat, packed, jnp.zeros((14, width), F32)], 0).astype(BF)
-
-
-def fit_kernel(lay, me_ref, came_ref, first_ref, out_ref):
-    third = lay.third
-    c = me_ref[2]
-    t0, t2, came = first_ref[:, :third], first_ref[:, third : 2 * third], came_ref[:, :third]
-    out_ref[:, : 3 * third] = jnp.where(c == 0, jnp.concatenate([t0, t2, came], 1), jnp.concatenate([came, t0, t2], 1))
-    out_ref[:, 3 * third :] = first_ref[:, 2 * third :]
+        ref[2 * band :] = jnp.concatenate([flat, jnp.zeros((15, width), F32)], 0).astype(BF)
+
+
+def fit_kernel(lay, came_ref, first_ref, out_ref):
+    third, rows = lay.third, lay.rows
+    c = here()[2]
+    t0, t2, came = first_ref[:rows, :third], first_ref[:rows, third : 2 * third], came_ref[:, :third]
+    out_ref[:rows, : 3 * third] = jnp.where(c == 0, jnp.concatenate([t0, t2, came], 1), jnp.concatenate([came, t0, t2], 1))
+    out_ref[:rows, 3 * third :] = first_ref[:rows, 2 * third :]
+    out_ref[rows:] = jnp.zeros((16, out_ref.shape[1]), BF)
+    out_ref[rows : rows + 1, :PACKED] = first_ref[rows : rows + 1, :PACKED]
+    out_ref[rows : rows + 1, PACKED : 2 * PACKED] = came_ref[0:1, came_ref.shape[1] - PACKED :]
 
 
 def merge_kernel(lay, *refs):
@@ -143,45 +166,68 @@
         bottom_ref[k] = ref[half:]
 
 
-def owner_mask(lay, devices, table_row, me_ref):
-    place = lax.broadcasted_iota(jnp.int32, (devices, 1), 0)
-    row_rel, img_place = place & 3, place >> 2
-    row = (((row_rel & 1) << 1) | (row_rel >> 1)) ^ me_ref[3]
-    img_rel = jnp.zeros_like(place)
-    for k, bit in enumerate(lay.high + [0]):
-        img_rel = img_rel | (((img_place >> k) & 1) << bit)
-    return ((img_rel ^ me_ref[0]) * 4 + row) == table_row
-
-
-def unpack_kernel(lay, plan, me_ref, v_ref, table_ref, out_ref):
-    c = me_ref[2]
-    devices = v_ref.shape[0]
+def join_kernel(lay, *refs):
+    for part in range(2):
+        near, far = refs[2 * part : 2 * part + 2]
+        refs[4 + part][: near.shape[0]] = near[...]
+        refs[4 + part][near.shape[0] :] = far[...]
+
+
+def owner_mask(lay, c_rel, table_row):
+    place = lax.broadcasted_iota(jnp.int32, (2 * lay.img_count, 1), 0)
+    row = here()[3] ^ (((place >> (lay.bits - 1)) & 1) * 2 + c_rel)
+    img_rel = place >> lay.bits
+    for k, bit in enumerate(lay.high):
+        img_rel = img_rel | (((place >> k) & 1) << bit)
+    return ((img_rel ^ here()[0]) * 4 + row) == table_row
+
+
+def owners(table_ref, at, c):
+    owner = jnp.where(c == 0, table_ref[0:1, at], table_ref[2:3, at])
+    entry = jnp.where(c == 0, table_ref[1:2, at], table_ref[3:4, at])
+    return owner, entry
+
+
+def unpack_kernel(lay, plan, n_v, table_ref, *refs):
+    v_refs, out_ref = refs[:n_v], refs[n_v]
+    if lay.aligned:
+        half = lay.half_rows
+        gathered = jnp.concatenate([ref[k, half : half + 16][0:1] for ref in v_refs for k in range(ref.shape[0])], 0)
+    else:
+        gathered = v_refs[0][...]
     for start, size, offset, count in plan:
         at = slice(start, start + size)
-        owner = jnp.where(c == 0, table_ref[0:1, at], table_ref[2:3, at])
-        entry = jnp.where(c == 0, table_ref[1:2, at], table_ref[3:4, at])
-        place = lax.broadcasted_iota(jnp.int32, (count, size), 0)
-        spread = (place == entry).astype(F32).astype(BF)
-        rows = nn(v_ref[:, offset : offset + count], spread)
-        out_ref[:, at] = column_sum(jnp.where(owner_mask(lay, devices, owner, me_ref), rows, 0.0))
-
-
-def repack_kernel(lay, plan, me_ref, table_ref, *refs):
-    grads, out_ref = refs[:-1], refs[-1]
-    c = me_ref[2]
-    devices = out_ref.shape[0]
-    out_ref[...] = jnp.zeros_like(out_ref)
-    for ref, (start, size, offset, count) in zip(grads, plan):
-        at = slice(start, start + size)
-        owner = jnp.where(c == 0, table_ref[0:1, at], table_ref[2:3, at])
-        entry = jnp.where(c == 0, table_ref[1:2, at], table_ref[3:4, at])
-        place = lax.broadcasted_iota(jnp.int32, (count, size), 0)
-        spread = (place == entry).astype(F32).astype(BF)
-        rows = jnp.where(owner_mask(lay, devices, owner, me_ref), ref[...], 0.0).astype(BF)
-        out_ref[:, offset : offset + count] = nt(rows, spread)
-
-
-def project_kernel(lay, n_w, me_ref, t0, t1, t2, t3, *refs):
+        owner, entry = owners(table_ref, at, here()[2])
+        spread = (lax.broadcasted_iota(jnp.int32, (count, size), 0) == entry).astype(F32).astype(BF)
+        total = 0.0
+        for c_rel in range(2):
+            rows = nn(gathered[:, c_rel * PACKED + offset : c_rel * PACKED + offset + count], spread)
+            total = total + column_sum(jnp.where(owner_mask(lay, c_rel, owner), rows, 0.0))
+        out_ref[:, at] = total
+
+
+def repack(lay, plan, table_ref, grads, refs):
+    sides = []
+    for c_rel in range(2):
+        parts = []
+        for grad, (start, size, offset, count) in zip(grads, plan):
+            owner, entry = owners(table_ref, slice(start, start + size), here()[2])
+            spread = (lax.broadcasted_iota(jnp.int32, (count, size), 0) == entry).astype(F32).astype(BF)
+            rows = jnp.where(owner_mask(lay, c_rel, owner), grad, 0.0).astype(BF)
+            parts.append(nt(rows, spread))
+        used = sum(p.shape[1] for p in parts)
+        sides += parts + [jnp.zeros((2 * lay.img_count, PACKED - used), F32)]
+    rows = jnp.concatenate(sides, 1)
+    if not lay.aligned:
+        refs[1][...] = rows.astype(BF)
+        return
+    half, count = lay.half_rows, lay.img_count
+    for j in range(2 * count):
+        block = jnp.concatenate([rows[j : j + 1], jnp.zeros((15, rows.shape[1]), F32)], 0).astype(BF)
+        refs[2 + j // count][j % count, half : half + 16, :] = block
+
+
+def project_kernel(lay, n_w, t0, t1, t2, t3, *refs):
     w_refs = refs[:n_w]
     vec_ref, a_ref, q_ref, k_ref, v_ref, w_out, p_out, cos_ref, sin_ref, kp_ref, bias_ref, w_all = refs[n_w:]
     band, side, own, third = lay.band, lay.side, lay.own, lay.third
@@ -200,7 +246,7 @@
     sign = jnp.where((lane & (lay.head // 2)) == 0, -1.0, 1.0).astype(F32)
     col = lax.broadcasted_iota(jnp.int32, (side, own), 0).astype(F32) * f_ref[:, :own]
     col_cos, col_sin = jnp.cos(col), jnp.sin(col)
-    row_index = me_ref[3]
+    row_index = here()[3]
     for b, flip in enumerate((0, 2, 1, 3)):
         first = ((row_index ^ flip) * lay.band_rows).astype(F32)
         rows = (lax.broadcasted_iota(jnp.int32, (8, own), 0).astype(F32) + first) * f_ref[:, own:]
@@ -212,8 +258,8 @@
             sin_ref[at] = (col_sin * rc + col_cos * rs) * sign
     block = lay.width // 4
     for y_rel in range(2):
-        y_side = me_ref[1] ^ y_rel
-        load_pieces(lay, me_ref, w_refs, y_rel, w_all.at[y_side])
+        y_side = here()[1] ^ y_rel
+        load_pieces(lay, w_refs, y_rel, w_all.at[y_side])
     acts = a_ref[...]
     w0, w1 = w_all[0].reshape(lay.width, -1), w_all[1].reshape(lay.width, -1)
     p_out[:, :block], p_out[:, block:] = w0[:, 3 * third :], w1[:, 3 * third :]
@@ -254,9 +300,9 @@
     lax.fori_loop(0, HEADS // 4, step, 0)
 
 
-def middle_kernel(lay, me_ref, t0, t1, t2, t3, ob_ref, oo_ref, p_ref, po_ref, vec_ref, x1_ref, a2_ref, wp_ref):
+def middle_kernel(lay, t0, t1, t2, t3, ob_ref, oo_ref, p_ref, po_ref, vec_ref, x1_ref, a2_ref, wp_ref):
     band, third, half = lay.band, lay.third, lay.length // 2
-    c = me_ref[2]
+    c = here()[2]
     block = lay.width // 4
     pb_ref, g_ref, s_ref = (vec_ref[:, lay.at[n]] for n in ("proj_bias", "mlp_gain", "mlp_shift"))
     for y_side in range(2):
@@ -278,7 +324,7 @@
         a2_ref[at] = (normed * g_ref + s_ref).astype(BF)
 
 
-def mlp_kernel(lay, n_w, n_g, chunk, me_ref, t0, t1, t2, t3, kp_ref, x1_ref, a2_ref, *refs):
+def mlp_kernel(lay, n_w, n_g, chunk, t0, t1, t2, t3, kp_ref, x1_ref, a2_ref, *refs):
     w_refs = refs[:n_w]
     vec_ref, part_ref, msend_ref, dn_ref, dnsend_ref, ubg_ref, dbg_ref = refs[n_w : n_w + 7]
     grads = refs[n_w + 7 : n_w + 7 + n_g]
@@ -296,12 +342,12 @@
     shape = lay.tiles + (chunk,)
 
     for y_rel in range(2):
-        load_pieces(lay, me_ref, w_refs, y_rel, w_all)
+        load_pieces(lay, w_refs, y_rel, w_all)
 
         def step(n, carry, y_rel=y_rel):
             at = pl.ds(pl.multiple_of(n * chunk, chunk), chunk)
             d_at = pl.ds(pl.multiple_of(n * chunk + width, chunk), chunk)
-            b_at = n * chunk + (me_ref[1] ^ y_rel) * width
+            b_at = n * chunk + (here()[1] ^ y_rel) * width
             up = w_all[:, :, at].reshape(width, chunk)
             down = w_all[:, :, d_at].reshape(width, chunk)
             acts = a2_ref[...]
@@ -315,9 +361,9 @@
             m_ref[...] += nt(act, down)
             dn_ref[...] += nt(du, up)
             g_tmp[...] = nn(at_ref[...], du).astype(BF).reshape(shape)
-            store_pieces(lay, me_ref, grads, y_rel, at, g_tmp)
+            store_pieces(lay, grads, y_rel, at, g_tmp)
             g_tmp[...] = nn(dt_ref[...], act).astype(BF).reshape(shape)
-            store_pieces(lay, me_ref, grads, y_rel, d_at, g_tmp)
+            store_pieces(lay, grads, y_rel, d_at, g_tmp)
             return carry
 
         lax.fori_loop(0, width // chunk, step, 0)
@@ -327,15 +373,15 @@
 
 
 def back_kernel(
-    lay, n_g, chunk, me_ref, t0, t1, t2, t3, kp_ref, x1_ref, dn_ref, came_ref, vec_ref, wp_ref, ob_ref, oo_ref, q_ref, k_ref, v_ref,
-    p_ref, cos_ref, sin_ref, a_ref, *refs,
+    lay, plan, n_g, chunk, t0, t1, t2, t3, kp_ref, x1_ref, dn_ref, came_ref, vec_ref, wp_ref, ob_ref, oo_ref, q_ref, k_ref, v_ref,
+    p_ref, cos_ref, sin_ref, a_ref, w_ref, table_ref, ubg_ref, dbg_ref, *refs,
 ):
-    dx_ref, pbg_ref, gg_ref, sg_ref, bqk_ref, bv_ref, fg_ref, dqkv_ref = refs[:8]
-    grads = refs[8 : 8 + n_g]
-    dxb_ref, dob_ref, dq_ref, dk_ref, dv_ref, g_tmp = refs[8 + n_g :]
+    dx_ref, keep_ref, send_ref = refs[:3]
+    grads = refs[3 : 3 + n_g]
+    dxb_ref, dob_ref, dq_ref, dk_ref, dv_ref, g_tmp, dqkv_ref = refs[3 + n_g :]
     g_ref = vec_ref[:, lay.at["mlp_gain"]]
     band, side, own, third, half, head = lay.band, lay.side, lay.own, lay.third, lay.length // 2, lay.head
-    c = me_ref[2]
+    c = here()[2]
     pair = 2 * head
     scale = head**-0.5
     gg, sg, pbg = 0.0, 0.0, 0.0
@@ -352,7 +398,6 @@
             gg = gg + column_sum(dn * normed)
             sg = sg + column_sum(dn)
             pbg = pbg + column_sum(dxb.astype(F32))
-    gg_ref[...], sg_ref[...], pbg_ref[...] = gg, sg, pbg
     low = [pl.ds(pl.multiple_of((2 * s + c) * third, third), third) for s in range(2)]
     own_w = jnp.concatenate([wp_ref[low[0]], wp_ref[low[1]]], 0)
     dxb = dxb_ref[...]
@@ -405,7 +450,7 @@
     by_col = jnp.zeros((side, own), F32)
     by_row = jnp.zeros((side, own), F32)
     for b, flip in enumerate((0, 2, 1, 3)):
-        first = ((me_ref[3] ^ flip) * lay.band_rows).astype(F32)
+        first = ((here()[3] ^ flip) * lay.band_rows).astype(F32)
         for r in range(lay.band_rows):
             turn = dq_ref[b * band + r * side : b * band + (r + 1) * side]
             by_col = by_col + turn
@@ -415,31 +460,33 @@
     place = lax.broadcasted_iota(jnp.int32, (side, own), 0).astype(F32)
     both = jnp.concatenate([column_sum(by_col * place), column_sum(by_row)], 0) * sign
     both = jnp.where(sign < 0, both + halves_of(lay, both), 0.0)
-    fg_ref[:, :own], fg_ref[:, own:] = both[0:1], both[1:2]
-    bqk_ref[...] = column_sum(dqkv_ref[:, : 2 * own].astype(F32))
-    bv_ref[...] = column_sum(dqkv_ref[:, 2 * own :].astype(F32))
+    freqs = jnp.concatenate([both[0:1], both[1:2]], 1)
+    bqk = column_sum(dqkv_ref[:, : 2 * own].astype(F32))
+    bv = column_sum(dqkv_ref[:, 2 * own :].astype(F32))
+    grad = nt(dqkv_ref[:, : 3 * third], w_ref[0]) + nt(dqkv_ref[:, 3 * third :], w_ref[1])
+    keep_ref[...] = grad[:half]
+    send_ref[...] = grad[half:].astype(BF)
+    g1, s1 = 0.0, 0.0
+    for b, ref in enumerate((t0, t1, t2, t3)):
+        part = grad[b * band : (b + 1) * band]
+        normed, _ = normed_rows(ref[:band].astype(F32))
+        g1 = g1 + column_sum(part * normed)
+        s1 = s1 + column_sum(part)
+    repack(lay, plan, table_ref, [bqk, bv, pbg, g1, s1, gg, sg, ubg_ref[...], dbg_ref[...], freqs], grads)
     acts = a_ref[...]
     sides = []
     for y_side in range(2):
         grad = tn(acts, dqkv_ref[:, y_side * 3 * third : (y_side + 1) * 3 * third]).astype(BF)
         sides.append(jnp.concatenate([grad, p_grad[:, y_side * block : (y_side + 1) * block]], 1))
-    y = me_ref[1]
+    y = here()[1]
     for y_rel in range(2):
         g_tmp[...] = jnp.where((y ^ y_rel) == 0, sides[0], sides[1]).reshape(g_tmp.shape)
-        store_pieces(lay, me_ref, grads, y_rel, slice(None), g_tmp)
-
-
-def last_kernel(lay, dqkv_ref, w_ref, keep_ref, send_ref):
-    third, half = lay.third, lay.length // 2
-    grad = nt(dqkv_ref[:, : 3 * third], w_ref[0]) + nt(dqkv_ref[:, 3 * third :], w_ref[1])
-    keep_ref[...] = grad[:half]
-    send_ref[...] = grad[half:].astype(BF)
-
-
-def finish_kernel(lay, t0, t1, keep_ref, came_ref, dx_ref, vec_ref, out_ref, send_ref, gg_ref, sg_ref):
+        store_pieces(lay, grads, y_rel, slice(None), g_tmp)
+
+
+def finish_kernel(lay, t0, t1, keep_ref, came_ref, dx_ref, vec_ref, out_ref, send_ref):
     band = lay.band
     g_ref = vec_ref[:, lay.at["attn_gain"]]
-    gg, sg = 0.0, 0.0
     for b, ref in enumerate((t0, t1)):
         at = slice(b * band, (b + 1) * band)
         dn = keep_ref[at] + came_ref[at].astype(F32)
@@ -449,22 +496,43 @@
             out_ref[...] = result
         else:
             send_ref[...] = result
-        gg = gg + column_sum(dn * normed)
-        sg = sg + column_sum(dn)
-    gg_ref[...], sg_ref[...] = gg, sg
-
-
-def call(kernel, name, inputs, outs, scratch=(), smem=1, limit=16, us=1):
+
+
+def tail_send_kernel(lay, sum_ref, out_ref):
+    third, rows = lay.third, lay.rows
+    out_ref[:, :third] = jnp.where(here()[2] == 0, sum_ref[:rows, 2 * third : 3 * third], sum_ref[:rows, :third])
+    out_ref[:, third:] = jnp.zeros((rows, out_ref.shape[1] - third), BF)
+    out_ref[0:1, out_ref.shape[1] - PACKED :] = sum_ref[rows : rows + 1, PACKED : 2 * PACKED]
+
+
+def tail_kernel(lay, plan, sum_ref, came_ref, qkv_ref, proj_ref, *outs):
+    third, rows = lay.third, lay.rows
+    d0, d1, d2 = (sum_ref[:rows, k * third : (k + 1) * third] for k in range(3))
+    c = here()[2]
+    qkv_ref[:, :third] = jnp.where(c == 0, d0, d1).astype(F32)
+    qkv_ref[:, third : 2 * third] = came_ref[:, :third].astype(F32)
+    qkv_ref[:, 2 * third :] = jnp.where(c == 0, d1, d2).astype(F32)
+    proj_ref[...] = sum_ref[:rows, 3 * third :].astype(F32)
+    total = sum_ref[rows : rows + 1, :PACKED].astype(F32) + came_ref[0:1, came_ref.shape[1] - PACKED :].astype(F32)
+    for ref, (_, _, offset, count) in zip(outs, plan):
+        ref[...] = total[:, offset : offset + count]
+
+
+def call(kernel, name, inputs, outs, scratch=(), limit=16, hbm=False):
     return pl.pallas_call(
         kernel,
         out_shape=[jax.ShapeDtypeStruct(shape, dtype) for shape, dtype in outs],
-        in_specs=[SMEM] * smem + [VMEM] * (len(inputs) - smem),
+        in_specs=[HBM if hbm else VMEM] * len(inputs),
         out_specs=[VMEM] * len(outs),
-        scratch_shapes=[pltpu.VMEM(shape, dtype) for shape, dtype in scratch],
+        scratch_shapes=[s if not isinstance(s, tuple) else pltpu.VMEM(*s) for s in scratch],
         compiler_params=pltpu.CompilerParams(vmem_limit_bytes=limit * MIB),
-        cost_estimate=pl.CostEstimate(flops=us * 1000000000, bytes_accessed=1024, transcendentals=0),
+        cost_estimate=pl.CostEstimate(flops=1000, bytes_accessed=1024, transcendentals=0),
         name=name,
     )(*inputs)
+
+
+def after(value, *others):
+    return lax.optimization_barrier((value, *others))[0]
 
 
 class Slice:
@@ -474,7 +542,6 @@
         self.row = lax.axis_index("row")
         self.y = self.row // 2
         self.c = self.row % 2
-        self.facts = jnp.stack([self.img, self.y, self.c, self.row]).astype(jnp.int32)
         self.orders = (lay.high + [0, "y"], lay.high + ["y", 0])
 
     def swap(self, array, step):
@@ -510,36 +577,49 @@
         place = self.places(order).reshape(-1)
         return jnp.zeros_like(place).at[place].set(jnp.arange(place.size, dtype=jnp.int32))
 
-    def gather_rows(self, piece, name):
+    def gather_rows(self, piece, name, joined=False, early=lambda pieces: pieces, late=lambda pieces: pieces):
         lay = self.lay
         if not lay.aligned:
+            extra = [] if piece.shape[0] == lay.rows else [self.gather(piece[lay.rows], self.orders[1])]
+            piece = piece[: lay.rows]
             base = self.gather(piece, lay.high)
             whole = []
             for part, order in enumerate(self.orders):
                 held = base[:, part * lay.half_rows : (part + 1) * lay.half_rows]
                 held = self.gather(held, order[-2:]).reshape((-1,) + held.shape[1:])
                 whole.append(jnp.take(held, self.places(order), axis=0))
-            return [jnp.concatenate(whole, 2).reshape((2,) + lay.tiles + piece.shape[1:])]
+            return [jnp.concatenate(whole, 2).reshape((2,) + lay.tiles + piece.shape[1:])] + extra
         pieces = [piece]
         for step in lay.high:
             pieces += [self.swap(p, step) for p in pieces]
-        shape = (len(pieces), lay.half_rows, piece.shape[1])
-        halves = call(functools.partial(merge_kernel, lay), name, pieces, [(shape, BF)] * 2, smem=0)
-        parts = []
-        for order, held in zip(self.orders, halves):
-            near = self.swap(held, order[-2])
-            parts += [held, near, self.swap(held, order[-1]), self.swap(near, order[-1])]
-        return parts
-
-    def grad_shapes(self, columns):
+            pieces = early(pieces)
+        shapes = [((len(pieces), rows, piece.shape[1]), BF) for rows in (lay.half_rows, piece.shape[0] - lay.half_rows)]
+        halves = call(functools.partial(merge_kernel, lay), name, pieces, shapes)
+        near = [self.swap(held, order[-2]) for order, held in zip(self.orders, halves)]
+        if joined:
+            shapes = [((2 * h.shape[0],) + h.shape[1:], BF) for h in halves]
+            halves = call(functools.partial(join_kernel, lay), name, late([halves[0], near[0], halves[1], near[1]]), shapes)
+            parts = [[held, self.swap(held, order[-1])] for order, held in zip(self.orders, halves)]
+        else:
+            parts = [
+                [held, came, self.swap(held, order[-1]), self.swap(came, order[-1])]
+                for order, held, came in zip(self.orders, halves, near)
+            ]
+        return parts[0] + parts[1]
+
+    def grad_shapes(self, columns, extra=0):
         lay = self.lay
         if lay.aligned:
-            return [((lay.img_count, lay.half_rows, columns), BF)] * 4
-        return [((2,) + lay.tiles + (columns,), BF)]
+            return [((lay.img_count, lay.half_rows + more, columns), BF) for more in (0, 0, extra, extra)]
+        return [((2,) + lay.tiles + (columns,), BF)] + [((2 * lay.img_count, columns), BF)] * (extra > 0)
 
     def scatter_rows(self, parts):
         lay = self.lay
+        extra = []
         if not lay.aligned:
+            if len(parts) > 1:
+                row = self.scatter(parts[1], self.orders[1])[None]
+                extra = [jnp.pad(row, ((0, 15), (0, 0)))]
             pieces = parts[0].reshape(2, lay.img_count, lay.rows, parts[0].shape[3])
             parts = []
             for part, order in enumerate(self.orders):
@@ -552,7 +632,8 @@
             held = (keep.astype(F32) + self.swap(send, order[-1]).astype(F32)).astype(BF)
             half = lay.img_count // 2
             sums.append((held[:half].astype(F32) + self.swap(held[half:], order[-2]).astype(F32)).astype(BF))
-        return self.scatter(jnp.concatenate(sums, 1), lay.high)
+        total = self.scatter(jnp.concatenate(sums, 1), lay.high)
+        return jnp.concatenate([total] + extra, 0) if extra else total
 
 
 NAMES = ("qkv_bias", "proj_bias", "attn_gain", "attn_shift", "mlp_gain", "mlp_shift", "up_bias", "down_bias", "freqs")
@@ -599,14 +680,13 @@
     ):
         lay = Layout(img_count, tokens, qkv_weight.shape[0])
         me = Slice(lay)
-        y, c, facts = me.y, me.c, me.facts
+        y = me.y
         images, band, width, length = lay.images, lay.band, lay.width, lay.length
         heads = HEADS // 2
         own, third = lay.own, lay.third
         half = length // 2
         block = proj_weight.shape[1]
         hidden = up_weight.shape[1]
-        devices = img_count * 4
         vectors = (qkv_bias, proj_bias, attn_gain, attn_shift, mlp_gain, mlp_shift, up_bias, down_bias, rope_freqs)
         (plan, table), (grad_plan, grad_table) = plan_vectors(lay)
 
@@ -619,85 +699,87 @@
         pack_rows = 2 * band + 16
         mine, other, third_send, first_piece, second_piece = kernel(
             pack_kernel, "pack",
-            [facts, tokens.reshape(images, band, width), cotangent.reshape(images, band, width), keep_mask, qkv_weight, proj_weight,
+            [tokens.reshape(images, band, width), cotangent.reshape(images, band, width), keep_mask, qkv_weight, proj_weight,
              up_weight, down_weight.T, *[v.reshape(1, -1) for v in vectors]],
-            [((pack_rows, width), BF), ((pack_rows, width), BF), ((lay.rows, 2 * 128), BF), ((lay.rows, 2 * third + block), BF),
-             ((lay.rows, 2 * hidden), BF)], limit=12,
+            [((pack_rows, width), BF), ((pack_rows, width), BF), ((lay.rows, 256 + PACKED), BF),
+             ((lay.rows + 16, 2 * third + block), BF), ((lay.rows, 2 * hidden), BF)],
+            [(keep_mask.shape, jnp.int32), (qkv_weight.shape, F32), (proj_weight.shape, F32), (up_weight.shape, F32),
+             (down_weight.T.shape, F32), *[((1, v.shape[0]), F32) for v in vectors], pltpu.SemaphoreType.DMA((18,))],
+            limit=60, hbm=True,
         )
         third_came = me.swap(third_send, "c")
         near = me.swap(other, "y")
         bands = [mine, near, me.swap(mine, "c"), me.swap(near, "c")]
-        (first_piece,) = kernel(fit_kernel, "fit", [facts, third_came, first_piece], [((lay.rows, 3 * third + block), BF)])
-        first = me.gather_rows(first_piece, "merge_first")
-        second = me.gather_rows(second_piece, "merge_second")
-        held = jnp.concatenate([b[2 * band + 1 : 2 * band + 2] for b in bands], 0)[None]
-        vec_order = lay.high + [0]
-        for step in vec_order:
-            held = jnp.concatenate([held, me.swap(held, step)], 0)
+        (first_piece,) = kernel(fit_kernel, "fit", [third_came, first_piece], [((lay.rows + 16, 3 * third + block), BF)])
+        marks = {}
+
+        def note_first(pieces):
+            if len(pieces) == img_count // 2:
+                marks["high"] = pieces[1]
+                pieces[0] = after(pieces[0], near)
+            return pieces
+
+        first = me.gather_rows(first_piece, "merge_first", early=note_first)
+        if lay.aligned:
+            second_piece = after(second_piece, marks["high"])
+            first_near = (first[1], first[5])
+
+        def hold_second(pieces):
+            if len(pieces) == 2:
+                pieces[1] = after(pieces[1], *first_near)
+            return pieces
+
+        second = me.gather_rows(second_piece, "merge_second", True, hold_second)
+        first, vec_parts = (first, first[4:]) if lay.aligned else (first[:1], first[1:])
         (vec,) = call(
-            functools.partial(unpack_kernel, lay, plan), "unpack", [facts, held.reshape(devices, width), table],
+            functools.partial(unpack_kernel, lay, plan, len(vec_parts)), "unpack", [table, *vec_parts],
             [((1, table.shape[1]), F32)], limit=24,
         )
 
-        n_w = len(first)
+        n_w, n_s = len(first), len(second)
         n_g = len(me.grad_shapes(1))
         a1, q, k, v, w_qkv, p_cols, cos, sin, kp, mask_bias = call(
-            functools.partial(project_kernel, lay, n_w), "qkv", [facts, *bands, *first, vec],
+            functools.partial(project_kernel, lay, n_w), "qkv", [*bands, *first, vec],
             [((length, width), BF), ((length, own), BF), ((length, own), BF), ((length, own), BF), ((2, width, 3 * third), BF),
              ((width, 2 * block), BF), ((length, own), F32), ((length, own), F32), ((length, 1), F32), ((1, length), F32)],
-            [((2,) + lay.tiles + (3 * third + block,), BF)], limit=24, us=5,
+            [((2,) + lay.tiles + (3 * third + block,), BF)], limit=16,
         )
         p_other = me.swap(p_cols, "c")
         ob, p = call(
             functools.partial(attend_kernel, lay, band), "attend", [q, k, v, mask_bias],
-            [((length, own), BF), ((heads, length, length), BF)], smem=0, limit=12, us=11,
+            [((length, own), BF), ((heads, length, length), BF)], limit=8,
         )
         ob_other = me.swap(ob, "c")
         x1, a2, w_proj = call(
-            functools.partial(middle_kernel, lay), "middle", [facts, *bands, ob, ob_other, p_cols, p_other, vec],
-            [((length, width), F32), ((length, width), BF), ((width, width), BF)], limit=16, us=3,
+            functools.partial(middle_kernel, lay), "middle", [*bands, ob, ob_other, p_cols, p_other, vec],
+            [((length, width), F32), ((length, width), BF), ((width, width), BF)], limit=10,
         )
         part, m_send, dn, dn_send, d_up_bias, d_down_bias, *second_grads = call(
-            functools.partial(mlp_kernel, lay, n_w, n_g, 256), "mlp", [facts, *bands, kp, x1, a2, *second, vec],
+            functools.partial(mlp_kernel, lay, n_s, n_g, 256), "mlp", [*bands, kp, x1, a2, *second, vec],
             [((half, width), F32), ((half, width), BF), ((length, width), F32), ((length, width), BF), ((1, 2 * hidden), F32),
              ((1, width), F32), *me.grad_shapes(2 * hidden)],
             [((length, width), BF), ((width, length), BF), ((width, length), BF), ((length, width), F32),
-             (lay.tiles + (2 * hidden,), BF), (lay.tiles + (256,), BF)], limit=32, us=24,
+             (lay.tiles + (2 * hidden,), BF), (lay.tiles + (256,), BF)], limit=18,
         )
         d_second = me.scatter_rows(second_grads)
         dn_came = me.swap(dn_send, "c")
         m_came = me.swap(m_send, "c")
         out_half = (kp[:half] * (part + m_came.astype(F32))).astype(BF)
-        dx_half, d_proj_bias, d_g2, d_s2, d_qk_bias, d_v_bias, d_freqs, dqkv, *first_grads = call(
-            functools.partial(back_kernel, lay, n_g, band), "back",
-            [facts, *bands, kp, x1, dn, dn_came, vec, w_proj, ob, ob_other, q, k, v, p, cos, sin, a1],
-            [((half, width), F32), ((1, width), F32), ((1, width), F32), ((1, width), F32), ((1, 2 * own), F32), ((1, own), F32),
-             ((1, 2 * own), F32), ((length, 3 * own), BF), *me.grad_shapes(3 * third + block)],
+        grad_shapes = me.grad_shapes(3 * third + block, 16)
+        dx_half, dn1_keep, dn1_send, *first_grads = call(
+            functools.partial(back_kernel, lay, grad_plan, len(grad_shapes), band), "back",
+            [*bands, kp, x1, dn, dn_came, vec, w_proj, ob, ob_other, q, k, v, p, cos, sin, a1, w_qkv, grad_table, d_up_bias,
+             d_down_bias],
+            [((half, width), F32), ((half, width), F32), ((half, width), BF), *grad_shapes],
             [((length, width), BF), ((length, own), BF), ((length, own), F32), ((length, own), F32), ((length, own), F32),
-             (lay.tiles + (3 * third + block,), BF)], limit=32, us=24,
+             (lay.tiles + (3 * third + block,), BF), ((length, 3 * own), BF)], limit=24,
         )
         d_first = me.scatter_rows(first_grads)
-        dn1_keep, dn1_send = call(
-            functools.partial(last_kernel, lay), "last", [dqkv, w_qkv], [((half, width), F32), ((half, width), BF)], smem=0, us=2
-        )
         dn1_came = me.swap(dn1_send, "c")
-        tg_keep, tg_send, d_g1, d_s1 = call(
+        tg_keep, tg_send = call(
             functools.partial(finish_kernel, lay), "finish", [bands[0], bands[1], dn1_keep, dn1_came, dx_half, vec],
-            [((band, width), BF), ((band, width), BF), ((1, width), F32), ((1, width), F32)], smem=0,
-        )
-
-        grads = [d_qk_bias, d_v_bias, d_proj_bias, d_g1, d_s1, d_g2, d_s2, d_up_bias, d_down_bias, d_freqs]
-        sums = call(
-            functools.partial(repack_kernel, lay, grad_plan), "repack", [facts, grad_table, *grads], [((devices, 384), F32)],
-            limit=24,
-        )[0].reshape(img_count, 4, 384)
-        for step in reversed(vec_order):
-            count = sums.shape[0] // 2
-            sums = sums[:count] + me.swap(sums[count:], step)
-        sums = sums[0]
-        sums = sums[:2] + me.swap(sums[2:], "c")
-        total = sums[0] + me.swap(sums[1], "y")
-        r = [total[offset : offset + count] for _, _, offset, count in grad_plan]
+            [((band, width), BF), ((band, width), BF)],
+        )
 
         def to_images(keep, send):
             came = me.swap(send, "y")
@@ -708,10 +790,13 @@
 
         d_up = d_second[:, :hidden].astype(F32)
         d_down = d_second[:, hidden:].T.astype(F32)
-        d0, d1, d2 = d_first[:, :third], d_first[:, third : 2 * third], d_first[:, 2 * third : 3 * third]
-        came = me.swap(pick(c, d2, d0), "c")
-        d_qkv = pick(c, jnp.concatenate([d0, came, d1], 1), jnp.concatenate([d1, came, d2], 1)).astype(F32)
-        d_proj = d_first[:, 3 * third :].astype(F32)
+        (tail_send,) = kernel(tail_send_kernel, "tail_send", [d_first], [((lay.rows, 256 + PACKED), BF)])
+        tail_came = me.swap(tail_send, "c")
+        d_qkv, d_proj, *r = call(
+            functools.partial(tail_kernel, lay, grad_plan), "tail", [d_first, tail_came],
+            [((lay.rows, 3 * third), F32), ((lay.rows, block), F32), *[((1, count), F32) for _, _, _, count in grad_plan]],
+        )
+        r = [v.reshape(-1) for v in r]
         return (
             layer_out, tokens_grad, d_qkv, r[0], r[1], d_proj, r[2], r[3], r[4], r[5], r[6], d_up, r[7], d_down, r[8], r[9],
         )

time: 285 us -> 245 us (0.86)
  local copies, waits for them, and re-layouts: 32.6 us -> 4.08 us
  starting transfers between devices: 51.7 us -> 45.9 us
  Pallas kernels: 60.9 us -> 57.2 us
    unnamed x137 -> x23, local copies, waits for them, and re-layouts: 28.8 us -> 2.99 us
    ppermute x26 -> x19, waiting for transfers between devices: 83.6 us -> 89 us  [swap(): lax.ppermute(array, 'img', [(i, i ^ 1 << step) for i in range(self.lay.im...]
    ppermute x14 -> x12, waiting for transfers between devices: 39.8 us -> 35.7 us  [swap(): return lax.ppermute(array, 'row', [(r, r ^ 2) for r in range(4)])]
    pallas_call x13 -> x14, Pallas kernels: 60.9 us -> 57.2 us  [call(): pl.pallas_call(kernel, out_shape=[jax.ShapeDtypeStruct(shape, dtype) for...]
    ppermute x26 -> x19, starting transfers between devices: 34.6 us -> 31.7 us  [swap(): lax.ppermute(array, 'img', [(i, i ^ 1 << step) for i in range(self.lay.im...]
    ppermute x14 -> x12, starting transfers between devices: 15.5 us -> 12.6 us  [swap(): return lax.ppermute(array, 'row', [(r, r ^ 2) for r in range(4)])]
  transfers between devices with their start and end apart: 50 -> 40, of which waited for: 22 -> 20; matrix products, arithmetic and copies ran while one was open for 5% -> 4% of each run, Pallas kernels for 8% -> 16%
where the time goes in v1:
time: 245 us; the launch traced here: 244 us
  waiting for transfers between devices  127 us (52%)
  Pallas kernels  57.2 us (23%)
  starting transfers between devices  45.9 us (19%)
  other arithmetic  9.42 us (4%)
  local copies, waits for them, and re-layouts  4.08 us (2%)
    ppermute x19, waiting for transfers between devices, swap(): lax.ppermute(array, 'img', [(i, i ^ 1 << step) for i in range(self.lay.im...  89 us
    pallas_call x14, Pallas kernels, call(): pl.pallas_call(kernel, out_shape=[jax.ShapeDtypeStruct(shape, dtype) for...  57.2 us
    ppermute x12, waiting for transfers between devices, swap(): return lax.ppermute(array, 'row', [(r, r ^ 2) for r in range(4)])  35.7 us
    ppermute x19, starting transfers between devices, swap(): lax.ppermute(array, 'img', [(i, i ^ 1 << step) for i in range(self.lay.im...  31.7 us
    ppermute x12, starting transfers between devices, swap(): return lax.ppermute(array, 'row', [(r, r ^ 2) for r in range(4)])  12.6 us
  transfers between devices with their start and end apart: 40, of which 20 were waited for; matrix products, arithmetic and copies ran while one was open for 4% of the time, Pallas kernels for 16%

profile of v1, /device:TPU:0, one launch (start us, length us, event | category | flops | bytes accessed | tf_op | source)
XLA Modules:
  0.0 244.4 jit_solution(4935366292361076665)
XLA Ops:
  0.6 1.3 copy.35.refs_2_
  1.9 2.9 %pack.1 = (bf16[304,768]{1,0:T(8,128)(2,1)}, bf16[304,768]{1,0:T(8,128)(2,1)}, bf16[96,640]{1,0:T(8,128)(2,1)}, bf16[112,576]{1,0:T(8,128)(2,1)}, bf16[96,1536]{1,0:T(8,128)(2,1)}) custom-call(bf16[2,144,768]{2,1,0:T(8,128)(2,1)} %bitcast.34, bf16[2,144,768]{2,1,0:T(8,128)(2,1)} %bitcast.35, s32[2,6,24]{2,1,0:T(8,128)} %copy.35.refs_2_, f32[96,576]{1,0:T(8,128)} %refs_3_.1, ...), custom_call_target="tpu_custom_call" | custom-call | flops 1000 | bytes 1024 | tf_op jit(solution)/shard_map/pack/pallas_call | solution.py:522
  5.3 2.6 %collective-permute-start = (bf16[304,768]{1,0:T(8,128)(2,1)}, bf16[304,768]{1,0:T(8,128)(2,1)S(1)}, u32[]{:S(2)}, u32[]{:S(2)}) collective-permute-start(bf16[304,768]{1,0:T(8,128)(2,1)} %get-tuple-element.77), channel_id=1, source_target_pairs={{0,2},{1,3},{2,0},{3,1},{4,6},{5,7},{6,4},{7,5},{8,10},{9,11},{10,... | collective-permute-start | bytes 1400840 | tf_op jit(solution)/shard_map/ppermute | solution.py:551
  7.9 0.9 copy-done.2
  9.0 2.7 %collective-permute-start.4 = (bf16[112,768]{1,0:T(8,128)(2,1)S(1)}, bf16[112,768]{1,0:T(8,128)(2,1)S(1)}, u32[]{:S(2)}, u32[]{:S(2)}) collective-permute-start(bf16[112,768]{1,0:T(8,128)(2,1)S(1)} %fit.1.refs_0_), channel_id=1, source_target_pairs={{0,16},{4,20},{8,24},{12,28},{16,0},{20,4},{24,8},{28,12},{1,17},{... | collective-permute-start | bytes 516104 | tf_op jit(solution)/shard_map/ppermute | solution.py:552
  11.6 1.6 collective-permute-start.5
  13.2 7.0 %collective-permute-done.4.refs_1_ = bf16[112,768]{1,0:T(8,128)(2,1)S(1)} collective-permute-done((bf16[112,768]{1,0:T(8,128)(2,1)S(1)}, bf16[112,768]{1,0:T(8,128)(2,1)S(1)}, u32[]{:S(2)}, u32[]{:S(2)}) %collective-permute-start.4) | collective-permute-done | bytes 172064 | tf_op jit(solution)/shard_map/ppermute | solution.py:552
  20.8 5.0 %collective-permute-done.6.refs_3_ = bf16[112,768]{1,0:T(8,128)(2,1)S(1)} collective-permute-done((bf16[112,768]{1,0:T(8,128)(2,1)S(1)}, bf16[112,768]{1,0:T(8,128)(2,1)S(1)}, u32[]{:S(2)}, u32[]{:S(2)}) %collective-permute-start.6) | collective-permute-done | bytes 172064 | tf_op jit(solution)/shard_map/ppermute | solution.py:552
  25.8 1.5 collective-permute-start.10
  27.3 3.0 %collective-permute-start.15 = (bf16[96,1536]{1,0:T(8,128)(2,1)}, bf16[96,1536]{1,0:T(8,128)(2,1)S(1)}, u32[]{:S(2)}, u32[]{:S(2)}) collective-permute-start(bf16[96,1536]{1,0:T(8,128)(2,1)} %get-tuple-element.93.refs_0_), channel_id=1, source_target_pairs={{0,16},{4,20},{8,24},{12,28},{16,0},{20,4},{24,8},{28,12},{1,17},{... | collective-permute-start | bytes 884744 | tf_op jit(solution)/shard_map/ppermute | solution.py:552
  30.3 1.5 collective-permute-start.7
  31.8 1.7 collective-permute-start.16
  33.5 9.8 %collective-permute-done.15.refs_1_ = bf16[96,1536]{1,0:T(8,128)(2,1)S(1)} collective-permute-done((bf16[96,1536]{1,0:T(8,128)(2,1)}, bf16[96,1536]{1,0:T(8,128)(2,1)S(1)}, u32[]{:S(2)}, u32[]{:S(2)}) %collective-permute-start.15) | collective-permute-done | bytes 294944 | tf_op jit(solution)/shard_map/ppermute | solution.py:552
  44.9 6.3 %collective-permute-done.17.refs_3_ = bf16[96,1536]{1,0:T(8,128)(2,1)S(1)} collective-permute-done((bf16[96,1536]{1,0:T(8,128)(2,1)S(1)}, bf16[96,1536]{1,0:T(8,128)(2,1)S(1)}, u32[]{:S(2)}, u32[]{:S(2)}) %collective-permute-start.17) | collective-permute-done | bytes 294944 | tf_op jit(solution)/shard_map/ppermute | solution.py:552
  51.3 1.6 collective-permute-start.18
  54.1 1.5 collective-permute-start.12
  55.6 12.1 %collective-permute-done.18.refs_1_ = bf16[4,48,1536]{2,1,0:T(8,128)(2,1)S(1)} collective-permute-done((bf16[4,48,1536]{2,1,0:T(8,128)(2,1)S(1)}, bf16[4,48,1536]{2,1,0:T(8,128)(2,1)S(1)}, u32[]{:S(2)}, u32[]{:S(2)}) %collective-permute-start.18) | collective-permute-done | bytes 589856 | tf_op jit(solution)/shard_map/ppermute | solution.py:552
  68.5 1.5 collective-permute-start.21
  70.0 6.1 %collective-permute-done.11.refs_2_.refs_6_ = bf16[4,64,768]{2,1,0:T(8,128)(2,1)S(1)} collective-permute-done((bf16[4,64,768]{2,1,0:T(8,128)(2,1)S(1)}, bf16[4,64,768]{2,1,0:T(8,128)(2,1)S(1)}, u32[]{:S(2)}, u32[]{:S(2)}) %collective-permute-start.11) | collective-permute-done | bytes 393248 | tf_op jit(solution)/shard_map/ppermute | solution.py:552
  76.7 7.8 %collective-permute-done.12.refs_3_.refs_7_ = bf16[4,64,768]{2,1,0:T(8,128)(2,1)S(1)} collective-permute-done((bf16[4,64,768]{2,1,0:T(8,128)(2,1)S(1)}, bf16[4,64,768]{2,1,0:T(8,128)(2,1)S(1)}, u32[]{:S(2)}, u32[]{:S(2)}) %collective-permute-start.12) | collective-permute-done | bytes 393248 | tf_op jit(solution)/shard_map/ppermute | solution.py:552
  85.6 15.2 %collective-permute-done.8.refs_2_ = bf16[4,48,768]{2,1,0:T(8,128)(2,1)S(1)} collective-permute-done((bf16[4,48,768]{2,1,0:T(8,128)(2,1)S(1)}, bf16[4,48,768]{2,1,0:T(8,128)(2,1)S(1)}, u32[]{:S(2)}, u32[]{:S(2)}) %collective-permute-start.8) | collective-permute-done | bytes 294944 | tf_op jit(solution)/shard_map/ppermute | solution.py:551
  100.9 3.2 %collective-permute-done.9.refs_3_ = bf16[4,48,768]{2,1,0:T(8,128)(2,1)S(1)} collective-permute-done((bf16[4,48,768]{2,1,0:T(8,128)(2,1)S(1)}, bf16[4,48,768]{2,1,0:T(8,128)(2,1)S(1)}, u32[]{:S(2)}, u32[]{:S(2)}) %collective-permute-start.9) | collective-permute-done | bytes 294944 | tf_op jit(solution)/shard_map/ppermute | solution.py:551
  104.0 3.1 %qkv.1 = (bf16[576,768]{1,0:T(8,128)(2,1)S(1)}, bf16[576,384]{1,0:T(8,128)(2,1)S(1)}, bf16[576,384]{1,0:T(8,128)(2,1)S(1)}, bf16[576,384]{1,0:T(8,128)(2,1)S(1)}...) custom-call(bf16[304,768]{1,0:T(8,128)(2,1)S(1)} %copy-done, ...), custom_call_target="tpu_custom_call" | custom-call | flops 1000 | bytes 1024 | tf_op jit(solution)/shard_map/qkv/pallas_call | solution.py:522
  107.2 10.5 %attend.1 = (bf16[576,384]{1,0:T(8,128)(2,1)S(1)}, bf16[6,576,576]{2,1,0:T(8,128)(2,1)S(1)}) custom-call(bf16[576,384]{1,0:T(8,128)(2,1)S(1)} %get-tuple-element.84.q_ref, bf16[576,384]{1,0:T(8,128)(2,1)S(1)} %get-tuple-element.85.k_ref, bf16[576,384]{1,0:T(8,128)(2,1)S(1)} %get-tuple-element.86.v_ref, f32[1,576]{1,0:T(1,128)S(1)} %get-tuple-element.87.bias_ref), custom_call_target="tpu_custom_call" | custom-call | flops 1000 | bytes 1024 | tf_op jit(solution)/shard_map/attend/pallas_call | solution.py:522
  118.1 1.5 collective-permute-done.13.oo_ref
  119.6 2.0 middle.1
  121.6 13.8 %mlp.1 = (f32[288,768]{1,0:T(8,128)S(1)}, bf16[288,768]{1,0:T(8,128)(2,1)S(1)}, f32[576,768]{1,0:T(8,128)S(1)}, bf16[576,768]{1,0:T(8,128)(2,1)S(1)}, f32[1,1536...) custom-call(bf16[304,768]{1,0:T(8,128)(2,1)S(1)} %copy-done, ...), custom_call_target="tpu_custom_call" | custom-call | flops 1000 | bytes 1024 | tf_op jit(solution)/shard_map/mlp/pallas_call | solution.py:522
  138.8 1.5 collective-permute-start.23
  140.2 22.5 %back.1 = (f32[288,768]{1,0:T(8,128)S(1)}, f32[288,768]{1,0:T(8,128)S(1)}, bf16[288,768]{1,0:T(8,128)(2,1)}, bf16[8,48,768]{2,1,0:T(8,128)(2,1)S(1)}, bf16[8,48,...) custom-call(bf16[304,768]{1,0:T(8,128)(2,1)S(1)} %copy-done, ...), custom_call_target="tpu_custom_call" | custom-call | flops 1000 | bytes 1024 | tf_op jit(solution)/shard_map/back/pallas_call | solution.py:522
  163.3 0.9 collective-permute-start.29
  164.7 1.1 collective-permute-start.35
  166.1 14.9 %collective-permute-done.27 = bf16[8,48,768]{2,1,0:T(8,128)(2,1)S(1)} collective-permute-done((bf16[8,48,768]{2,1,0:T(8,128)(2,1)S(1)}, bf16[8,48,768]{2,1,0:T(8,128)(2,1)S(1)}, u32[]{:S(2)}, u32[]{:S(2)}) %collective-permute-start.27) | collective-permute-done | bytes 589856 | tf_op jit(solution)/shard_map/ppermute | solution.py:551
  181.8 1.9 collective-permute-done.29
  183.8 0.9 collective-permute-start.28
  184.9 11.5 %collective-permute-done.35 = bf16[4,48,1536]{2,1,0:T(8,128)(2,1)S(1)} collective-permute-done((bf16[4,48,1536]{2,1,0:T(8,128)(2,1)S(1)}, bf16[4,48,1536]{2,1,0:T(8,128)(2,1)S(1)}, u32[]{:S(2)}, u32[]{:S(2)}) %collective-permute-start.35) | collective-permute-done | bytes 589856 | tf_op jit(solution)/shard_map/ppermute | solution.py:552
  196.4 1.5 collective-permute-start.30
  198.2 0.9 pad_maximum_fusion
  199.1 3.2 %collective-permute-start.38 = (bf16[2,96,1536]{2,1,0:T(8,128)(2,1)}, bf16[2,96,1536]{2,1,0:T(8,128)(2,1)}, u32[]{:S(2)}, u32[]{:S(2)}) collective-permute-start(bf16[2,96,1536]{2,1,0:T(8,128)(2,1)} %pad_maximum_fusion), channel_id=1, source_target_pairs={{0,8},{4,12},{8,0},{12,4},{16,24},{20,28},{24,16},{28,20},{1,9},{5... | collective-permute-start | bytes 1769480 | tf_op jit(solution)/shard_map/ppermute | solution.py:552
  202.4 2.3 collective-permute-done.30
  206.3 3.2 %collective-permute-start.31 = (bf16[2,112,768]{2,1,0:T(8,128)(2,1)}, bf16[2,112,768]{2,1,0:T(8,128)(2,1)}, u32[]{:S(2)}, u32[]{:S(2)}) collective-permute-start(bf16[2,112,768]{2,1,0:T(8,128)(2,1)} %pad_maximum_fusion.1), channel_id=1, source_target_pairs={{0,8},{4,12},{8,0},{12,4},{16,24},{20,28},{24,16},{28,20},{1,9},{5... | collective-permute-start | bytes 1032200 | tf_op jit(solution)/shard_map/ppermute | solution.py:552
  209.6 2.1 maximum_select_fusion
  212.3 1.4 collective-permute-start.26
  213.7 6.7 %collective-permute-done.31 = bf16[2,112,768]{2,1,0:T(8,128)(2,1)} collective-permute-done((bf16[2,112,768]{2,1,0:T(8,128)(2,1)}, bf16[2,112,768]{2,1,0:T(8,128)(2,1)}, u32[]{:S(2)}, u32[]{:S(2)}) %collective-permute-start.31) | collective-permute-done | bytes 344096 | tf_op jit(solution)/shard_map/ppermute | solution.py:552
  220.5 1.1 add_convert_fusion.8
  221.5 4.7 %collective-permute-start.32 = (bf16[1,112,768]{2,1,0:T(8,128)(2,1)S(1)}, bf16[1,112,768]{2,1,0:T(8,128)(2,1)S(1)}, u32[]{:S(2)}, u32[]{:S(2)}) collective-permute-start(bf16[1,112,768]{2,1,0:T(8,128)(2,1)S(1)} %slice.93), channel_id=1, source_target_pairs={{0,16},{4,20},{8,24},{12,28},{16,0},{20,4},{24,8},{28,12},{1,17},{... | collective-permute-start | bytes 516104 | tf_op jit(solution)/shard_map/ppermute | solution.py:552
  226.2 1.2 add_convert_fusion.3
  227.6 11.0 %collective-permute-done.32 = bf16[1,112,768]{2,1,0:T(8,128)(2,1)S(1)} collective-permute-done((bf16[1,112,768]{2,1,0:T(8,128)(2,1)S(1)}, bf16[1,112,768]{2,1,0:T(8,128)(2,1)S(1)}, u32[]{:S(2)}, u32[]{:S(2)}) %collective-permute-start.32) | collective-permute-done | bytes 172064 | tf_op jit(solution)/shard_map/ppermute | solution.py:552
  239.6 2.8 %collective-permute-done.39 = bf16[1,96,1536]{2,1,0:T(8,128)(2,1)S(1)} collective-permute-done((bf16[1,96,1536]{2,1,0:T(8,128)(2,1)S(1)}, bf16[1,96,1536]{2,1,0:T(8,128)(2,1)S(1)}, u32[]{:S(2)}, u32[]{:S(2)}) %collective-permute-start.39) | collective-permute-done | bytes 294944 | tf_op jit(solution)/shard_map/ppermute | solution.py:552
  (95 shorter events, 18.3 us)
Async XLA Ops:
  4.8 46.4 %copy-start.1 = (bf16[96,1536]{1,0:T(8,128)(2,1)S(1)}, bf16[96,1536]{1,0:T(8,128)(2,1)}, u32[]{:S(2)}) copy-start(bf16[96,1536]{1,0:T(8,128)(2,1)} %get-tuple-element.93.refs_0_) | copy-start | bytes 884740
  4.8 48.7 %copy-start = (bf16[304,768]{1,0:T(8,128)(2,1)S(1)}, bf16[304,768]{1,0:T(8,128)(2,1)}, u32[]{:S(2)}) copy-start(bf16[304,768]{1,0:T(8,128)(2,1)} %get-tuple-element.76.t0) | copy-start | bytes 1400836
  4.8 3.1 %collective-permute-start.3 = (bf16[96,640]{1,0:T(8,128)(2,1)}, bf16[96,640]{1,0:T(8,128)(2,1)S(1)}, u32[]{:S(2)}, u32[]{:S(2)}) collective-permute-start(bf16[96,640]{1,0:T(8,128)(2,1)} %get-tuple-element.78), channel_id=1, source_target_pairs={{0,1},{1,0},{2,3},{3,2},{4,5},{5,4},{6,7},{7,6},{8,9},{9,8},{10,11... | collective-permute-start | bytes 368648 | tf_op jit(solution)/shard_map/ppermute | solution.py:549
  5.3 15.4 %collective-permute-start = (bf16[304,768]{1,0:T(8,128)(2,1)}, bf16[304,768]{1,0:T(8,128)(2,1)S(1)}, u32[]{:S(2)}, u32[]{:S(2)}) collective-permute-start(bf16[304,768]{1,0:T(8,128)(2,1)} %get-tuple-element.77), channel_id=1, source_target_pairs={{0,2},{1,3},{2,0},{3,1},{4,6},{5,7},{6,4},{7,5},{8,10},{9,11},{10,... | collective-permute-start | bytes 1400840 | tf_op jit(solution)/shard_map/ppermute | solution.py:551
  9.0 11.2 %collective-permute-start.4 = (bf16[112,768]{1,0:T(8,128)(2,1)S(1)}, bf16[112,768]{1,0:T(8,128)(2,1)S(1)}, u32[]{:S(2)}, u32[]{:S(2)}) collective-permute-start(bf16[112,768]{1,0:T(8,128)(2,1)S(1)} %fit.1.refs_0_), channel_id=1, source_target_pairs={{0,16},{4,20},{8,24},{12,28},{16,0},{20,4},{24,8},{28,12},{1,17},{... | collective-permute-start | bytes 516104 | tf_op jit(solution)/shard_map/ppermute | solution.py:552
  11.6 9.1 %collective-permute-start.5 = (bf16[112,768]{1,0:T(8,128)(2,1)S(1)}, bf16[112,768]{1,0:T(8,128)(2,1)S(1)}, u32[]{:S(2)}, u32[]{:S(2)}) collective-permute-start(bf16[112,768]{1,0:T(8,128)(2,1)S(1)} %fit.1.refs_0_), channel_id=1, source_target_pairs={{0,8},{4,12},{8,0},{12,4},{16,24},{20,28},{24,16},{28,20},{1,9},{5... | collective-permute-start | bytes 516104 | tf_op jit(solution)/shard_map/ppermute | solution.py:552
  20.2 5.6 %collective-permute-start.6 = (bf16[112,768]{1,0:T(8,128)(2,1)S(1)}, bf16[112,768]{1,0:T(8,128)(2,1)S(1)}, u32[]{:S(2)}, u32[]{:S(2)}) collective-permute-start(bf16[112,768]{1,0:T(8,128)(2,1)S(1)} %collective-permute-done.4.refs_1_), channel_id=1, source_target_pairs={{0,8},{4,12},{8,0},{12,4},{16,24},{20,28},{24,16},{28,20},{1,9},{5... | collective-permute-start | bytes 516104 | tf_op jit(solution)/shard_map/ppermute | solution.py:552
  25.8 17.5 %collective-permute-start.10 = (bf16[4,64,768]{2,1,0:T(8,128)(2,1)S(1)}, bf16[4,64,768]{2,1,0:T(8,128)(2,1)S(1)}, u32[]{:S(2)}, u32[]{:S(2)}) collective-permute-start(bf16[4,64,768]{2,1,0:T(8,128)(2,1)S(1)} %get-tuple-element.82.refs_0_.refs_4_), channel_id=1, source_target_pairs={{0,2},{1,3},{2,0},{3,1},{4,6},{5,7},{6,4},{7,5},{8,10},{9,11},{10,... | collective-permute-start | bytes 1179656 | tf_op jit(solution)/shard_map/ppermute | solution.py:551
  27.3 16.0 %collective-permute-start.15 = (bf16[96,1536]{1,0:T(8,128)(2,1)}, bf16[96,1536]{1,0:T(8,128)(2,1)S(1)}, u32[]{:S(2)}, u32[]{:S(2)}) collective-permute-start(bf16[96,1536]{1,0:T(8,128)(2,1)} %get-tuple-element.93.refs_0_), channel_id=1, source_target_pairs={{0,16},{4,20},{8,24},{12,28},{16,0},{20,4},{24,8},{28,12},{1,17},{... | collective-permute-start | bytes 884744 | tf_op jit(solution)/shard_map/ppermute | solution.py:552
  30.3 13.0 %collective-permute-start.7 = (bf16[4,48,768]{2,1,0:T(8,128)(2,1)S(1)}, bf16[4,48,768]{2,1,0:T(8,128)(2,1)S(1)}, u32[]{:S(2)}, u32[]{:S(2)}) collective-permute-start(bf16[4,48,768]{2,1,0:T(8,128)(2,1)S(1)} %get-tuple-element.81.refs_0_), channel_id=1, source_target_pairs={{0,4},{4,0},{8,12},{12,8},{16,20},{20,16},{24,28},{28,24},{1,5},{5... | collective-permute-start | bytes 884744 | tf_op jit(solution)/shard_map/ppermute | solution.py:552
  31.8 13.2 %collective-permute-start.16 = (bf16[96,1536]{1,0:T(8,128)(2,1)}, bf16[96,1536]{1,0:T(8,128)(2,1)S(1)}, u32[]{:S(2)}, u32[]{:S(2)}) collective-permute-start(bf16[96,1536]{1,0:T(8,128)(2,1)} %get-tuple-element.93.refs_0_), channel_id=1, source_target_pairs={{0,8},{4,12},{8,0},{12,4},{16,24},{20,28},{24,16},{28,20},{1,9},{5... | collective-permute-start | bytes 884744 | tf_op jit(solution)/shard_map/ppermute | solution.py:552
  43.3 7.9 %collective-permute-start.17 = (bf16[96,1536]{1,0:T(8,128)(2,1)S(1)}, bf16[96,1536]{1,0:T(8,128)(2,1)S(1)}, u32[]{:S(2)}, u32[]{:S(2)}) collective-permute-start(bf16[96,1536]{1,0:T(8,128)(2,1)S(1)} %collective-permute-done.15.refs_1_), channel_id=1, source_target_pairs={{0,8},{4,12},{8,0},{12,4},{16,24},{20,28},{24,16},{28,20},{1,9},{5... | collective-permute-start | bytes 884744 | tf_op jit(solution)/shard_map/ppermute | solution.py:552
  51.3 16.3 %collective-permute-start.18 = (bf16[4,48,1536]{2,1,0:T(8,128)(2,1)S(1)}, bf16[4,48,1536]{2,1,0:T(8,128)(2,1)S(1)}, u32[]{:S(2)}, u32[]{:S(2)}) collective-permute-start(bf16[4,48,1536]{2,1,0:T(8,128)(2,1)S(1)} %get-tuple-element.95.refs_0_), channel_id=1, source_target_pairs={{0,4},{4,0},{8,12},{12,8},{16,20},{20,16},{24,28},{28,24},{1,5},{5... | collective-permute-start | bytes 1769480 | tf_op jit(solution)/shard_map/ppermute | solution.py:552
  52.9 14.8 %collective-permute-start.19 = (bf16[4,48,1536]{2,1,0:T(8,128)(2,1)S(1)}, bf16[4,48,1536]{2,1,0:T(8,128)(2,1)S(1)}, u32[]{:S(2)}, u32[]{:S(2)}) collective-permute-start(bf16[4,48,1536]{2,1,0:T(8,128)(2,1)S(1)} %get-tuple-element.96.refs_2_), channel_id=1, source_target_pairs={{0,2},{1,3},{2,0},{3,1},{4,6},{5,7},{6,4},{7,5},{8,10},{9,11},{10,... | collective-permute-start | bytes 1769480 | tf_op jit(solution)/shard_map/ppermute | solution.py:551
  53.5 31.6 %copy-start.4 = (s32[4,8064]{1,0:T(4,128)S(1)}, s32[4,8064]{1,0:T(4,128)}, u32[]{:S(2)}) copy-start(s32[4,8064]{1,0:T(4,128)} %constant.23.clone.table_ref) | copy-start | bytes 387076
  53.5 16.5 %collective-permute-start.1 = (bf16[304,768]{1,0:T(8,128)(2,1)S(1)}, bf16[304,768]{1,0:T(8,128)(2,1)S(1)}, u32[]{:S(2)}, u32[]{:S(2)}) collective-permute-start(bf16[304,768]{1,0:T(8,128)(2,1)S(1)} %copy-done), channel_id=1, source_target_pairs={{0,1},{1,0},{2,3},{3,2},{4,5},{5,4},{6,7},{7,6},{8,9},{9,8},{10,11... | collective-permute-start | bytes 1400840 | tf_op jit(solution)/shard_map/ppermute | solution.py:549
  53.5 22.6 %collective-permute-start.11 = (bf16[4,64,768]{2,1,0:T(8,128)(2,1)S(1)}, bf16[4,64,768]{2,1,0:T(8,128)(2,1)S(1)}, u32[]{:S(2)}, u32[]{:S(2)}) collective-permute-start(bf16[4,64,768]{2,1,0:T(8,128)(2,1)S(1)} %get-tuple-element.82.refs_0_.refs_4_), channel_id=1, source_target_pairs={{0,4},{4,0},{8,12},{12,8},{16,20},{20,16},{24,28},{28,24},{1,5},{5... | collective-permute-start | bytes 1179656 | tf_op jit(solution)/shard_map/ppermute | solution.py:552
  54.1 30.4 %collective-permute-start.12 = (bf16[4,64,768]{2,1,0:T(8,128)(2,1)S(1)}, bf16[4,64,768]{2,1,0:T(8,128)(2,1)S(1)}, u32[]{:S(2)}, u32[]{:S(2)}) collective-permute-start(bf16[4,64,768]{2,1,0:T(8,128)(2,1)S(1)} %collective-permute-done.10.refs_1_.refs_5_), channel_id=1, source_target_pairs={{0,4},{4,0},{8,12},{12,8},{16,20},{20,16},{24,28},{28,24},{1,5},{5... | collective-permute-start | bytes 1179656 | tf_op jit(solution)/shard_map/ppermute | solution.py:552
  67.8 53.7 %collective-permute-start.20 = (bf16[8,48,1536]{2,1,0:T(8,128)(2,1)S(1)}, bf16[8,48,1536]{2,1,0:T(8,128)(2,1)S(1)}, u32[]{:S(2)}, u32[]{:S(2)}) collective-permute-start(bf16[8,48,1536]{2,1,0:T(8,128)(2,1)S(1)} %get-tuple-element.97.refs_0_), channel_id=1, source_target_pairs={{0,2},{1,3},{2,0},{3,1},{4,6},{5,7},{6,4},{7,5},{8,10},{9,11},{10,... | collective-permute-start | bytes 3538952 | tf_op jit(solution)/shard_map/ppermute | solution.py:551
  68.5 53.1 %collective-permute-start.21 = (bf16[8,48,1536]{2,1,0:T(8,128)(2,1)S(1)}, bf16[8,48,1536]{2,1,0:T(8,128)(2,1)S(1)}, u32[]{:S(2)}, u32[]{:S(2)}) collective-permute-start(bf16[8,48,1536]{2,1,0:T(8,128)(2,1)S(1)} %get-tuple-element.98.refs_2_), channel_id=1, source_target_pairs={{0,4},{4,0},{8,12},{12,8},{16,20},{20,16},{24,28},{28,24},{1,5},{5... | collective-permute-start | bytes 3538952 | tf_op jit(solution)/shard_map/ppermute | solution.py:552
  70.0 30.9 %collective-permute-start.2 = (bf16[304,768]{1,0:T(8,128)(2,1)S(1)}, bf16[304,768]{1,0:T(8,128)(2,1)S(1)}, u32[]{:S(2)}, u32[]{:S(2)}) collective-permute-start(bf16[304,768]{1,0:T(8,128)(2,1)S(1)} %collective-permute-done.t1), channel_id=1, source_target_pairs={{0,1},{1,0},{2,3},{3,2},{4,5},{5,4},{6,7},{7,6},{8,9},{9,8},{10,11... | collective-permute-start | bytes 1400840 | tf_op jit(solution)/shard_map/ppermute | solution.py:549
  76.1 24.8 %collective-permute-start.8 = (bf16[4,48,768]{2,1,0:T(8,128)(2,1)S(1)}, bf16[4,48,768]{2,1,0:T(8,128)(2,1)S(1)}, u32[]{:S(2)}, u32[]{:S(2)}) collective-permute-start(bf16[4,48,768]{2,1,0:T(8,128)(2,1)S(1)} %get-tuple-element.81.refs_0_), channel_id=1, source_target_pairs={{0,2},{1,3},{2,0},{3,1},{4,6},{5,7},{6,4},{7,5},{8,10},{9,11},{10,... | collective-permute-start | bytes 884744 | tf_op jit(solution)/shard_map/ppermute | solution.py:551
  84.5 19.5 %collective-permute-start.9 = (bf16[4,48,768]{2,1,0:T(8,128)(2,1)S(1)}, bf16[4,48,768]{2,1,0:T(8,128)(2,1)S(1)}, u32[]{:S(2)}, u32[]{:S(2)}) collective-permute-start(bf16[4,48,768]{2,1,0:T(8,128)(2,1)S(1)} %collective-permute-done.7.refs_1_), channel_id=1, source_target_pairs={{0,2},{1,3},{2,0},{3,1},{4,6},{5,7},{6,4},{7,5},{8,10},{9,11},{10,... | collective-permute-start | bytes 884744 | tf_op jit(solution)/shard_map/ppermute | solution.py:551
  107.1 12.5 %collective-permute-start.14 = (bf16[768,384]{1,0:T(8,128)(2,1)S(1)}, bf16[768,384]{1,0:T(8,128)(2,1)S(1)}, u32[]{:S(2)}, u32[]{:S(2)}) collective-permute-start(bf16[768,384]{1,0:T(8,128)(2,1)S(1)} %get-tuple-element.89.p_ref), channel_id=1, source_target_pairs={{0,1},{1,0},{2,3},{3,2},{4,5},{5,4},{6,7},{7,6},{8,9},{9,8},{10,11... | collective-permute-start | bytes 1769480 | tf_op jit(solution)/shard_map/ppermute | solution.py:549
  117.7 1.9 collective-permute-start.13
  135.4 28.9 %collective-permute-start.34 = (bf16[8,48,1536]{2,1,0:T(8,128)(2,1)S(1)}, bf16[8,48,1536]{2,1,0:T(8,128)(2,1)S(1)}, u32[]{:S(2)}, u32[]{:S(2)}) collective-permute-start(bf16[8,48,1536]{2,1,0:T(8,128)(2,1)S(1)} %get-tuple-element.130), channel_id=1, source_target_pairs={{0,2},{1,3},{2,0},{3,1},{4,6},{5,7},{6,4},{7,5},{8,10},{9,11},{10,... | collective-permute-start | bytes 3538952 | tf_op jit(solution)/shard_map/ppermute | solution.py:551
  136.1 1.8 collective-permute-start.22
  136.1 4.1 %collective-permute-start.24 = (bf16[576,768]{1,0:T(8,128)(2,1)S(1)}, bf16[576,768]{1,0:T(8,128)(2,1)S(1)}, u32[]{:S(2)}, u32[]{:S(2)}) collective-permute-start(bf16[576,768]{1,0:T(8,128)(2,1)S(1)} %get-tuple-element.102), channel_id=1, source_target_pairs={{0,1},{1,0},{2,3},{3,2},{4,5},{5,4},{6,7},{7,6},{8,9},{9,8},{10,11... | collective-permute-start | bytes 2654216 | tf_op jit(solution)/shard_map/ppermute | solution.py:549
  136.6 28.1 %collective-permute-start.36 = (bf16[8,48,1536]{2,1,0:T(8,128)(2,1)S(1)}, bf16[8,48,1536]{2,1,0:T(8,128)(2,1)S(1)}, u32[]{:S(2)}, u32[]{:S(2)}) collective-permute-start(bf16[8,48,1536]{2,1,0:T(8,128)(2,1)S(1)} %get-tuple-element.132), channel_id=1, source_target_pairs={{0,4},{4,0},{8,12},{12,8},{16,20},{20,16},{24,28},{28,24},{1,5},{5... | collective-permute-start | bytes 3538952 | tf_op jit(solution)/shard_map/ppermute | solution.py:552
  137.9 2.4 copy-start.3
  138.8 70.8 %collective-permute-start.23 = (bf16[144,768]{1,0:T(8,128)(2,1)}, bf16[144,768]{1,0:T(8,128)(2,1)}, u32[]{:S(2)}, u32[]{:S(2)}) collective-permute-start(bf16[144,768]{1,0:T(8,128)(2,1)} %get-tuple-element.137), channel_id=1, source_target_pairs={{0,2},{1,3},{2,0},{3,1},{4,6},{5,7},{6,4},{7,5},{8,10},{9,11},{10,... | collective-permute-start | bytes 663560 | tf_op jit(solution)/shard_map/ppermute | solution.py:551
  162.7 18.3 %collective-permute-start.27 = (bf16[8,48,768]{2,1,0:T(8,128)(2,1)S(1)}, bf16[8,48,768]{2,1,0:T(8,128)(2,1)S(1)}, u32[]{:S(2)}, u32[]{:S(2)}) collective-permute-start(bf16[8,48,768]{2,1,0:T(8,128)(2,1)S(1)} %get-tuple-element.117), channel_id=1, source_target_pairs={{0,2},{1,3},{2,0},{3,1},{4,6},{5,7},{6,4},{7,5},{8,10},{9,11},{10,... | collective-permute-start | bytes 1769480 | tf_op jit(solution)/shard_map/ppermute | solution.py:551
  163.3 20.5 %collective-permute-start.29 = (bf16[8,64,768]{2,1,0:T(8,128)(2,1)S(1)}, bf16[8,64,768]{2,1,0:T(8,128)(2,1)S(1)}, u32[]{:S(2)}, u32[]{:S(2)}) collective-permute-start(bf16[8,64,768]{2,1,0:T(8,128)(2,1)S(1)} %get-tuple-element.119), channel_id=1, source_target_pairs={{0,4},{4,0},{8,12},{12,8},{16,20},{20,16},{24,28},{28,24},{1,5},{5... | collective-permute-start | bytes 2359304 | tf_op jit(solution)/shard_map/ppermute | solution.py:552
  164.3 47.4 %collective-permute-start.25 = (bf16[288,768]{1,0:T(8,128)(2,1)}, bf16[288,768]{1,0:T(8,128)(2,1)S(1)}, u32[]{:S(2)}, u32[]{:S(2)}) collective-permute-start(bf16[288,768]{1,0:T(8,128)(2,1)} %get-tuple-element.112), channel_id=1, source_target_pairs={{0,1},{1,0},{2,3},{3,2},{4,5},{5,4},{6,7},{7,6},{8,9},{9,8},{10,11... | collective-permute-start | bytes 1327112 | tf_op jit(solution)/shard_map/ppermute | solution.py:549
  164.7 31.7 %collective-permute-start.35 = (bf16[4,48,1536]{2,1,0:T(8,128)(2,1)S(1)}, bf16[4,48,1536]{2,1,0:T(8,128)(2,1)S(1)}, u32[]{:S(2)}, u32[]{:S(2)}) collective-permute-start(bf16[4,48,1536]{2,1,0:T(8,128)(2,1)S(1)} %slice.95), channel_id=1, source_target_pairs={{0,4},{4,0},{8,12},{12,8},{16,20},{20,16},{24,28},{28,24},{1,5},{5... | collective-permute-start | bytes 1769480 | tf_op jit(solution)/shard_map/ppermute | solution.py:552
  181.0 17.0 %collective-permute-start.37 = (bf16[4,48,1536]{2,1,0:T(8,128)(2,1)S(1)}, bf16[4,48,1536]{2,1,0:T(8,128)(2,1)S(1)}, u32[]{:S(2)}, u32[]{:S(2)}) collective-permute-start(bf16[4,48,1536]{2,1,0:T(8,128)(2,1)S(1)} %slice.97), channel_id=1, source_target_pairs={{0,2},{1,3},{2,0},{3,1},{4,6},{5,7},{6,4},{7,5},{8,10},{9,11},{10,... | collective-permute-start | bytes 1769480 | tf_op jit(solution)/shard_map/ppermute | solution.py:551
  183.8 18.6 %collective-permute-start.28 = (bf16[4,48,768]{2,1,0:T(8,128)(2,1)S(1)}, bf16[4,48,768]{2,1,0:T(8,128)(2,1)S(1)}, u32[]{:S(2)}, u32[]{:S(2)}) collective-permute-start(bf16[4,48,768]{2,1,0:T(8,128)(2,1)S(1)} %slice.87), channel_id=1, source_target_pairs={{0,4},{4,0},{8,12},{12,8},{16,20},{20,16},{24,28},{28,24},{1,5},{5... | collective-permute-start | bytes 884744 | tf_op jit(solution)/shard_map/ppermute | solution.py:552
  196.4 8.3 %collective-permute-start.30 = (bf16[4,64,768]{2,1,0:T(8,128)(2,1)S(1)}, bf16[4,64,768]{2,1,0:T(8,128)(2,1)S(1)}, u32[]{:S(2)}, u32[]{:S(2)}) collective-permute-start(bf16[4,64,768]{2,1,0:T(8,128)(2,1)S(1)} %slice.89), channel_id=1, source_target_pairs={{0,2},{1,3},{2,0},{3,1},{4,6},{5,7},{6,4},{7,5},{8,10},{9,11},{10,... | collective-permute-start | bytes 1179656 | tf_op jit(solution)/shard_map/ppermute | solution.py:551
  198.2 4.3 %copy-start.7 = (bf16[4,48,1536]{2,1,0:T(8,128)(2,1)}, bf16[4,48,1536]{2,1,0:T(8,128)(2,1)S(1)}, u32[]{:S(2)}) copy-start(bf16[4,48,1536]{2,1,0:T(8,128)(2,1)S(1)} %add_convert_fusion.4) | copy-start | bytes 1769476
  199.1 27.1 %collective-permute-start.38 = (bf16[2,96,1536]{2,1,0:T(8,128)(2,1)}, bf16[2,96,1536]{2,1,0:T(8,128)(2,1)}, u32[]{:S(2)}, u32[]{:S(2)}) collective-permute-start(bf16[2,96,1536]{2,1,0:T(8,128)(2,1)} %pad_maximum_fusion), channel_id=1, source_target_pairs={{0,8},{4,12},{8,0},{12,4},{16,24},{20,28},{24,16},{28,20},{1,9},{5... | collective-permute-start | bytes 1769480 | tf_op jit(solution)/shard_map/ppermute | solution.py:552
  206.3 14.1 %collective-permute-start.31 = (bf16[2,112,768]{2,1,0:T(8,128)(2,1)}, bf16[2,112,768]{2,1,0:T(8,128)(2,1)}, u32[]{:S(2)}, u32[]{:S(2)}) collective-permute-start(bf16[2,112,768]{2,1,0:T(8,128)(2,1)} %pad_maximum_fusion.1), channel_id=1, source_target_pairs={{0,8},{4,12},{8,0},{12,4},{16,24},{20,28},{24,16},{28,20},{1,9},{5... | collective-permute-start | bytes 1032200 | tf_op jit(solution)/shard_map/ppermute | solution.py:552
  211.7 8.8 %copy-start.10 = (bf16[4,64,768]{2,1,0:T(8,128)(2,1)S(1)}, bf16[4,64,768]{2,1,0:T(8,128)(2,1)}, u32[]{:S(2)}) copy-start(bf16[4,64,768]{2,1,0:T(8,128)(2,1)} %copy-done.9) | copy-start | bytes 1179652
  212.3 14.0 %copy-start.6 = (bf16[4,48,1536]{2,1,0:T(8,128)(2,1)S(1)}, bf16[4,48,1536]{2,1,0:T(8,128)(2,1)}, u32[]{:S(2)}) copy-start(bf16[4,48,1536]{2,1,0:T(8,128)(2,1)} %copy-done.5) | copy-start | bytes 1769476
  212.3 14.0 %copy-start.8 = (bf16[4,48,1536]{2,1,0:T(8,128)(2,1)S(1)}, bf16[4,48,1536]{2,1,0:T(8,128)(2,1)}, u32[]{:S(2)}) copy-start(bf16[4,48,1536]{2,1,0:T(8,128)(2,1)} %copy-done.7) | copy-start | bytes 1769476
  212.3 26.4 %collective-permute-start.26 = (bf16[144,768]{1,0:T(8,128)(2,1)S(1)}, bf16[144,768]{1,0:T(8,128)(2,1)S(1)}, u32[]{:S(2)}, u32[]{:S(2)}) collective-permute-start(bf16[144,768]{1,0:T(8,128)(2,1)S(1)} %get-tuple-element.115), channel_id=1, source_target_pairs={{0,2},{1,3},{2,0},{3,1},{4,6},{5,7},{6,4},{7,5},{8,10},{9,11},{10,... | collective-permute-start | bytes 663560 | tf_op jit(solution)/shard_map/ppermute | solution.py:551
  221.5 17.1 %collective-permute-start.32 = (bf16[1,112,768]{2,1,0:T(8,128)(2,1)S(1)}, bf16[1,112,768]{2,1,0:T(8,128)(2,1)S(1)}, u32[]{:S(2)}, u32[]{:S(2)}) collective-permute-start(bf16[1,112,768]{2,1,0:T(8,128)(2,1)S(1)} %slice.93), channel_id=1, source_target_pairs={{0,16},{4,20},{8,24},{12,28},{16,0},{20,4},{24,8},{28,12},{1,17},{... | collective-permute-start | bytes 516104 | tf_op jit(solution)/shard_map/ppermute | solution.py:552
  227.5 14.9 %collective-permute-start.39 = (bf16[1,96,1536]{2,1,0:T(8,128)(2,1)S(1)}, bf16[1,96,1536]{2,1,0:T(8,128)(2,1)S(1)}, u32[]{:S(2)}, u32[]{:S(2)}) collective-permute-start(bf16[1,96,1536]{2,1,0:T(8,128)(2,1)S(1)} %slice.101), channel_id=1, source_target_pairs={{0,16},{4,20},{8,24},{12,28},{16,0},{20,4},{24,8},{28,12},{1,17},{... | collective-permute-start | bytes 884744 | tf_op jit(solution)/shard_map/ppermute | solution.py:552
  239.6 3.8 %collective-permute-start.33 = (bf16[96,640]{1,0:T(8,128)(2,1)S(1)}, bf16[96,640]{1,0:T(8,128)(2,1)S(1)}, u32[]{:S(2)}, u32[]{:S(2)}) collective-permute-start(bf16[96,640]{1,0:T(8,128)(2,1)S(1)} %tail_send.1), channel_id=1, source_target_pairs={{0,1},{1,0},{2,3},{3,2},{4,5},{5,4},{6,7},{7,6},{8,9},{9,8},{10,11... | collective-permute-start | bytes 368648 | tf_op jit(solution)/shard_map/ppermute | solution.py:549
  (3 other events, 2.8 us)
